TPU v7x, 256 devices: a whole 4x4x8 slice. The times are simulated.
256 devices in a mesh: pipe: 8 (over x, core), ulys: 32 (over z, y).
Axes of the slice: x: 4, y: 4, z: 8, core: 2. Of those that a mesh axis runs over, the one named last changes fastest.
Arguments:
- activations: bfloat16 [8, 1024, 3072], P('pipe', 'ulys'), may hold values from -6 to 6
- patch_index: int32 [8], P('pipe'), may hold values from 0 to 11
- modulation: float32 [8, 3, 3072], P('pipe'), may hold values from -4 to 4
- qkv_weight: bfloat16 [8, 3072, 9216], P('pipe', None, 'ulys'), may hold values from -0.109375 to 0.109375
- out_weight: bfloat16 [8, 3072, 3072], P('pipe', 'ulys'), may hold values from -0.109375 to 0.109375
- stale_cache: bfloat16 [8, 32, 3072, 2, 384], P('pipe', 'ulys'), may hold values from -360 to 360
- id_cache: bfloat16 [8, 32, 6, 8, 2, 384], P('pipe', 'ulys'), may hold values from -360 to 360
- region_ids: int32 [8, 1024], P('pipe', 'ulys'), may hold values from 0 to 6
- id_counts: int32 [8, 6], P('pipe'), may hold values from 1 to 32, as said below
Outputs:
- next_activations: bfloat16 [8, 1024, 3072], P('pipe', 'ulys')
Inputs may be any that keep to these rules, and one draw needn't show every extreme that they name: `id_counts`: in every section some subject has exactly 32 live identity tokens.
All inputs are finite; a program needn't handle non-finite values.
Results may differ from a plain program's by a relative error of at most 0.0117.
The roundings to bfloat16 on the way count: a program that leaves them out, or rounds other values in their place, can miss the bound.
Values may be sent and summed in bfloat16 or wider, within the bound.
A program may use at most 128 MiB of HBM per device.

v0:
```python
import jax
import jax.numpy as jnp
from jax import lax
from jax.sharding import PartitionSpec as P

HD = 128
HPD = 3
GROUPS = 8
SUBJ = 6


NEG_BIG = -1e30


def from_partner(x, axis, apart):
    return lax.ppermute(x, axis, [(i, i ^ 1 << apart) for i in range(lax.axis_size(axis))])


def passed_along(x, axis, by):
    size = lax.axis_size(axis)
    return lax.ppermute(x, axis, [(i, (i + by) % size) for i in range(size)])


def order_pair(mine, other, rank, level, axis):
    upper = rank // 2**level % 2
    first = jnp.where(upper == 1, other, mine)
    second = jnp.where(upper == 1, mine, other)
    return jnp.concatenate([first, second], axis=axis)


def block_attend(queries, keys, values, mask, factor):
    scores = jnp.einsum("qhd,khd->qhk", queries, keys, preferred_element_type=jnp.float32) * factor
    if mask is None:
        peak = jnp.max(scores, axis=2)
        weights = jnp.exp(scores - peak[:, :, None])
    else:
        wide = mask[:, None, :]
        peak = jnp.max(jnp.where(wide, scores, NEG_BIG), axis=2)
        weights = jnp.where(wide, jnp.exp(jnp.where(wide, scores - peak[:, :, None], 0.0)), 0.0)
    total = jnp.sum(weights, axis=2)
    output = jnp.einsum(
        "qhk,khd->qhd", weights.astype(jnp.bfloat16), values, preferred_element_type=jnp.float32
    )
    return (peak, total, output)


def merge_parts(first, second):
    peak = jnp.maximum(first[0], second[0])
    weight_one = jnp.exp(first[0] - peak)
    weight_two = jnp.exp(second[0] - peak)
    total = first[1] * weight_one + second[1] * weight_two
    output = first[2] * weight_one[:, :, None, None] + second[2] * weight_two[:, :, None, None]
    return (peak, total, output)


def merge_both(first, second):
    return merge_parts(first[:3], second[:3]) + merge_parts(first[3:], second[3:])


def shards(
    activations,
    patch_index,
    modulation,
    qkv_weight,
    out_weight,
    stale_cache,
    id_cache,
    region_ids,
    id_counts,
):
    ksplit = lax.axis_size("ulys") // GROUPS
    nbits = ksplit.bit_length() - 1
    rank = lax.axis_index("ulys") % ksplit
    rows = activations[0]
    modul = modulation[0]
    lifted = rows.astype(jnp.float32)
    center = jnp.mean(lifted, axis=1, keepdims=True)
    spread = jnp.mean(jnp.square(lifted - center), axis=1, keepdims=True)
    normed = (lifted - center) * lax.rsqrt(spread + 1e-06)
    hidden = (normed * (1.0 + modul[1]) + modul[0]).astype(jnp.bfloat16)
    all_rows, all_regions = (
        lax.all_gather(hidden, "ulys", axis=0, tiled=True),
        lax.all_gather(region_ids[0].astype(jnp.bfloat16), "ulys", axis=0, tiled=True),
    )
    total_rows = all_rows.shape[0]
    weight = qkv_weight[0]
    block_dims = HD // ksplit
    pieces = jnp.dot(all_rows, weight, preferred_element_type=jnp.float32).astype(jnp.bfloat16)[
        :, None, :
    ]
    for level in range(nbits):
        partner = from_partner(pieces, "ulys", level)
        pieces = order_pair(pieces, partner, rank, level, 1)
    fields = (
        pieces.reshape(total_rows, ksplit, 3, HPD, block_dims)
        .transpose(2, 0, 3, 1, 4)
        .reshape(3, total_rows, HPD, HD)
    )
    queries = fields[0]
    stored = stale_cache[0, 0]
    span = stored.shape[0]
    old_keys = stored[:, 0].reshape(span, HPD, HD)
    old_values = stored[:, 1].reshape(span, HPD, HD)
    patch = patch_index[0]
    per_block = span // total_rows
    owner = patch // per_block
    offset = patch % per_block * total_rows
    keys = jnp.where(
        rank == owner, lax.dynamic_update_slice(old_keys, fields[1], (offset, 0, 0)), old_keys
    )
    values = jnp.where(
        rank == owner, lax.dynamic_update_slice(old_values, fields[2], (offset, 0, 0)), old_values
    )
    factor = HD ** (-0.5)
    query_block = min(512, total_rows)
    block_count = total_rows // query_block

    def attend_rows(query_rows):
        return block_attend(query_rows, keys, values, None, factor)

    peaks, totals, outputs = lax.map(
        attend_rows, queries.reshape(block_count, query_block, HPD, HD)
    )
    peaks = peaks.reshape(total_rows, HPD)
    totals = totals.reshape(total_rows, HPD)
    outputs = outputs.reshape(total_rows, HPD, ksplit, block_dims)
    guests = id_cache[0, 0]
    id_slots = guests.shape[1]
    guest_keys = guests[:, :, 0].reshape(SUBJ * id_slots, HPD, HD)
    guest_values = guests[:, :, 1].reshape(SUBJ * id_slots, HPD, HD)
    slot_index = jnp.arange(id_slots, dtype=jnp.int32) + rank * id_slots
    valid = slot_index[None, :] < id_counts[0][:, None]
    subject = jnp.arange(1, SUBJ + 1).astype(jnp.bfloat16)
    match = all_regions[:, None] == subject[None, :]
    mask = (match[:, :, None] & valid[None]).reshape(total_rows, SUBJ * id_slots)
    guest_peak, guest_total, guest_out = block_attend(
        queries, guest_keys, guest_values, mask, factor
    )
    guest_out = guest_out.reshape(total_rows, HPD, ksplit, block_dims)
    state = (peaks, totals, outputs, guest_peak, guest_total, guest_out)
    for level in range(nbits):
        partner = from_partner(state, "ulys", level)
        state = merge_both(state, partner)
    own_out = lax.dynamic_index_in_dim(state[2], rank, 2, keepdims=False)
    guest_final = lax.dynamic_index_in_dim(state[5], rank, 2, keepdims=False)
    own_final = own_out / state[1][:, :, None]
    guest_final = guest_final / jnp.maximum(state[4], 1.0)[:, :, None]
    mixed = (own_final + guest_final).astype(jnp.bfloat16).reshape(total_rows, HPD * block_dims)
    proj_weight = out_weight[0]
    added = lax.psum_scatter(
        jnp.dot(mixed, proj_weight, preferred_element_type=jnp.float32).astype(jnp.bfloat16),
        "ulys",
        scatter_dimension=0,
        tiled=True,
    ).astype(jnp.float32)
    result = (lifted + modul[2] * added).astype(jnp.bfloat16)
    return passed_along(result[None], "pipe", 1)


def solution(mesh):
    placed = (
        P("pipe", "ulys", None),
        P("pipe"),
        P("pipe", None, None),
        P("pipe", None, "ulys"),
        P("pipe", "ulys", None),
        P("pipe", "ulys", None, None, None),
        P("pipe", "ulys", None, None, None, None),
        P("pipe", "ulys"),
        P("pipe", None),
    )
    return jax.shard_map(
        shards, mesh=mesh, in_specs=placed, out_specs=P("pipe", "ulys", None), check_vma=False
    )
```

profile of v0, /device:TPU:1, one launch (start us, length us, event | category | flops | bytes accessed | tf_op | source)
XLA Modules:
  0.0 691.2 jit_solution(16643877722455908787)
XLA Ops:
  6.5 0.9 fusion.61
  7.4 1.1 convert_reduce_fusion
  8.5 1.2 fusion.31
  9.7 1.8 fusion.34
  11.5 92.3 %all-gather.3.cloned.1.call-done = bf16[1024,3072]{1,0:T(8,128)(2,1)} async-done(((bf16[32,3072]{1,0:T(8,128)(2,1)}), bf16[1024,3072]{1,0:T(8,128)(2,1)}) %all-gather.3.cloned.1.call-update) | async-done | bytes 6291472 | tf_op jit(solution)/shard_map/all_gather | solution.py:82
  103.8 4.8 fusion.21
  108.6 0.1 collective-permute-start
  109.5 12.4 %copy.15 = bf16[1,1,3072,2,384]{2,4,3,1,0:T(8,128)(2,1)} copy(bf16[1,1,3072,2,384]{4,3,2,1,0:T(2,128)(2,1)} %param.16) | data formatting | bytes 9437184 | tf_op args[5]
  122.2 0.6 dynamic-slice.4
  123.4 0.2 dynamic-update-slice.2
  123.7 58.1 %all-reduce = bf16[1024]{0:T(1024)(128)(2,1)S(1)} all-reduce(bf16[1024]{0:T(1024)(128)(2,1)S(1)} %dynamic-update-slice.2), channel_id=2, replica_groups=mesh['pipe'=8,'ulys'=32] {'ulys'}, use_global_device_ids=true, to_apply=%add | all-reduce | flops 1024 | bytes 4096
  182.0 1.1 pad_maximum_fusion.1
  183.1 0.4 slice_reduce_fusion
  183.6 0.1 bitcast_and_fusion
  183.7 4.9 fusion.59
  188.6 11.5 %collective-permute-done.1 = bf16[1024,2,288]{0,2,1:T(8,128)(2,1)S(1)} collective-permute-done((bf16[1024,2,288]{0,2,1:T(8,128)(2,1)}, bf16[1024,2,288]{0,2,1:T(8,128)(2,1)S(1)}, u32[]{:S(2)}, u32[]{:S(2)}) %collective-permute-start.1) | collective-permute-done | bytes 1179680 | tf_op jit(solution)/shard_map/ppermute | solution.py:16
  200.0 0.2 broadcast_select_fusion.1
  200.2 0.2 pad_maximum_fusion
  200.4 0.3 copy.36
  200.7 0.2 fusion.60
  201.0 3.3 select_dynamic-update-slice_fusion
  204.3 4.3 copy.17
  208.5 4.3 copy.18
  212.8 0.6 reshape_squeeze.15
  213.4 0.7 copy.16
  214.1 87.2 %while.14 = (s32[]{:T(128)}, f32[2,512,3]{1,2,0:T(4,128)S(1)}, f32[2,512,3]{1,2,0:T(4,128)S(1)}, f32[2,512,3,128]{1,0,3,2:T(2,128)}, bf16[2,512,3,128]{3,1,2,0:T...) while((s32[]{:T(128)}, f32[2,512,3]{1,2,0:T(4,128)S(1)}, ...), condition=%wide.region_5.6_spmd, body=%wide.region_2.5_spmd.sunk | while | flops 2453664768 | bytes 65724520 | solution.py:121
  214.1 9.5 %bitcast_reduce_fusion.2 = (f32[512,3]{0,1:T(4,128)S(1)}, f32[3,512,3072]{2,1,0:T(8,128)}) fusion(bf16[3072,3,128]{2,0,1:T(8,128)(2,1)} %get-tuple-element.185, bf16[2,512,3,128]{3,1,2,0:T(8,128)(2,1)S(1)} %get-tuple-element.184, s32[]{:T(128)} %get-tuple-element.171), kind=kOutput, calls=%fused_computation.1.clone.1 | convolution fusion | flops 1217395200 | bytes 21633028 | tf_op jit(solution)/shard_map/while/body/eval_jaxpr/qhd,khd->qhk/dot_general | solution.py:32
  223.6 9.6 %fusion.75 = f32[512,3]{0,1:T(4,128)S(1)} fusion(f32[3,512,3072]{2,1,0:T(8,128)} %get-tuple-element.158, f32[512,3]{0,1:T(4,128)S(1)} %get-tuple-element.159), kind=kLoop, calls=%fused_computation.4.clone.1 | loop fusion | flops 14154240 | bytes 18886656 | tf_op jit(solution)/shard_map/while/body/eval_jaxpr/reduce_sum | solution.py:40
  233.2 9.0 %fusion.76 = f32[1,512,3,128]{3,1,2,0:T(8,128)S(1)} fusion(bf16[3072,3,128]{2,0,1:T(8,128)(2,1)} %get-tuple-element.186, f32[3,512,3072]{2,1,0:T(8,128)} %get-tuple-element.158, f32[512,3]{0,1:T(4,128)S(1)} %get-tuple-element.159), kind=kOutput, calls=%fused_computation.8.clone.1 | convolution fusion | flops 1222115328 | bytes 22026240 | tf_op jit(solution)/shard_map/while/body/eval_jaxpr/qhk,khd->qhd/dot_general | solution.py:41
  242.2 0.6 copy.38
  242.7 15.0 %dynamic_update_slice.18 = f32[2,512,3,128]{1,0,3,2:T(2,128)} dynamic-update-slice(f32[2,512,3,128]{1,0,3,2:T(2,128)} %get-tuple-element.174, f32[1,512,3,128]{1,0,3,2:T(1,128)S(1)} %copy.38, s32[]{:T(128)} %get-tuple-element.171, s32[]{:T(128)} %constant.98.clone.1..sunk, s32[]{:T(128)} %constant.98.clone.1..sunk, s32[]{:T(128)} %constant.98.clone.1..sunk) | dynamic-update-slice | bytes 1572868 | tf_op jit(solution)/shard_map/while/body/jit(dynamic_update_index_in_dim)/dynamic_update_slice | solution.py:121
  257.7 9.5 %bitcast_reduce_fusion.2 = (f32[512,3]{0,1:T(4,128)S(1)}, f32[3,512,3072]{2,1,0:T(8,128)}) fusion(bf16[3072,3,128]{2,0,1:T(8,128)(2,1)} %get-tuple-element.185, bf16[2,512,3,128]{3,1,2,0:T(8,128)(2,1)S(1)} %get-tuple-element.184, s32[]{:T(128)} %get-tuple-element.171), kind=kOutput, calls=%fused_computation.1.clone.1 | convolution fusion | flops 1217395200 | bytes 21633028 | tf_op jit(solution)/shard_map/while/body/eval_jaxpr/qhd,khd->qhk/dot_general | solution.py:32
  267.2 9.6 %fusion.75 = f32[512,3]{0,1:T(4,128)S(1)} fusion(f32[3,512,3072]{2,1,0:T(8,128)} %get-tuple-element.158, f32[512,3]{0,1:T(4,128)S(1)} %get-tuple-element.159), kind=kLoop, calls=%fused_computation.4.clone.1 | loop fusion | flops 14154240 | bytes 18886656 | tf_op jit(solution)/shard_map/while/body/eval_jaxpr/reduce_sum | solution.py:40
  276.8 9.0 %fusion.76 = f32[1,512,3,128]{3,1,2,0:T(8,128)S(1)} fusion(bf16[3072,3,128]{2,0,1:T(8,128)(2,1)} %get-tuple-element.186, f32[3,512,3072]{2,1,0:T(8,128)} %get-tuple-element.158, f32[512,3]{0,1:T(4,128)S(1)} %get-tuple-element.159), kind=kOutput, calls=%fused_computation.8.clone.1 | convolution fusion | flops 1222115328 | bytes 22026240 | tf_op jit(solution)/shard_map/while/body/eval_jaxpr/qhk,khd->qhd/dot_general | solution.py:41
  285.7 0.6 copy.38
  286.3 15.0 %dynamic_update_slice.18 = f32[2,512,3,128]{1,0,3,2:T(2,128)} dynamic-update-slice(f32[2,512,3,128]{1,0,3,2:T(2,128)} %get-tuple-element.174, f32[1,512,3,128]{1,0,3,2:T(1,128)S(1)} %copy.38, s32[]{:T(128)} %get-tuple-element.171, s32[]{:T(128)} %constant.98.clone.1..sunk, s32[]{:T(128)} %constant.98.clone.1..sunk, s32[]{:T(128)} %constant.98.clone.1..sunk) | dynamic-update-slice | bytes 1572868 | tf_op jit(solution)/shard_map/while/body/jit(dynamic_update_index_in_dim)/dynamic_update_slice | solution.py:121
  301.3 2.6 reshape.154
  304.0 0.3 select_reduce_fusion
  304.3 0.4 fusion.42
  304.7 1.5 collective-permute-start.9
  306.2 0.3 collective-permute-start.2
  306.6 1.1 collective-permute-start.6
  307.7 0.2 fusion.29
  307.9 0.4 collective-permute-start.8
  308.3 48.7 %collective-permute-done.2 = f32[1024,3]{0,1:T(4,128)S(1)} collective-permute-done((f32[1024,3]{0,1:T(4,128)S(1)}, f32[1024,3]{0,1:T(4,128)S(1)}, u32[]{:S(2)}, u32[]{:S(2)}) %collective-permute-start.2) | collective-permute-done | bytes 12320 | tf_op jit(solution)/shard_map/ppermute | solution.py:16
  357.0 0.3 collective-permute-start.12
  357.3 2.7 collective-permute-done.12
  360.1 1.5 multiply_add_fusion.1
  361.6 0.3 collective-permute-start.5
  361.9 0.3 multiply_add_fusion
  362.2 2.8 collective-permute-start.11
  365.0 0.3 collective-permute-start.4
  365.3 2.7 collective-permute-start.7
  368.0 0.3 collective-permute-start.10
  368.2 52.7 %collective-permute-done.4 = f32[1024,3]{0,1:T(4,128)S(1)} collective-permute-done((f32[1024,3]{0,1:T(4,128)S(1)}, f32[1024,3]{0,1:T(4,128)S(1)}, u32[]{:S(2)}, u32[]{:S(2)}) %collective-permute-start.4) | collective-permute-done | bytes 12320 | tf_op jit(solution)/shard_map/ppermute | solution.py:16
  421.0 3.8 collective-permute-start.13
  424.8 1.7 collective-permute-done.13
  426.6 1.4 fusion.41
  428.0 4.5 convolution_convert_fusion
  432.5 241.7 %reduce-scatter.2.cloned.1.call-done = bf16[32,3072]{1,0:T(8,128)(2,1)} async-done(((bf16[1024,3072]{1,0:T(8,128)(2,1)}), bf16[32,3072]{1,0:T(8,128)(2,1)}) %reduce-scatter.2.cloned.1.call-update) | async-done | bytes 196624 | tf_op jit(solution)/shard_map/reduce_scatter | solution.py:150
  674.3 1.0 fusion.47
  675.3 5.8 collective-permute-start.14
  681.0 2.6 collective-permute-done.14
  683.6 0.7 copy.59
  (55 shorter events, 0.9 us)
Async XLA Ops:
  6.5 97.2 %copy-start = (bf16[1,3072,288]{1,2,0:T(8,128)(2,1)S(1)}, bf16[1,3072,288]{1,2,0:T(8,128)(2,1)}, u32[]{:S(2)}) copy-start(bf16[1,3072,288]{1,2,0:T(8,128)(2,1)} %param.14) | copy-start | bytes 5308420
  6.5 97.2 %all-gather.3.cloned.1.call-start = ((), (), s32[]{:S(2)}) async-start(), calls=%async_computation.1 | async-start | bytes 6488064 | tf_op jit(solution)/shard_map/all_gather | solution.py:82
  11.4 662.8 %reduce-scatter.2.cloned.1.call-start = ((), (), s32[]{:S(2)}) async-start(), calls=%async_computation.2 | async-start | bytes 6488064 | tf_op jit(solution)/shard_map/reduce_scatter | solution.py:150
  108.6 73.3 %collective-permute-start = (bf16[1024,1,288]{0,2,1:T(8,128)(2,1)S(1)}, bf16[1024,1,288]{0,2,1:T(8,128)(2,1)S(1)}, u32[]{:S(2)}, u32[]{:S(2)}) collective-permute-start(bf16[1024,1,288]{0,2,1:T(8,128)(2,1)S(1)} %fusion.21), channel_id=1, source_target_pairs={{0,1},{1,0},{2,3},{3,2},{4,5},{5,4},{6,7},{7,6},{8,9},{9,8},{10,11... | collective-permute-start | bytes 1769480 | tf_op jit(solution)/shard_map/ppermute | solution.py:16
  109.5 12.5 %copy-start.5 = (s32[1,6]{1,0:T(1,128)S(1)}, s32[1,6]{1,0:T(1,128)}, u32[]{:S(2)}) copy-start(s32[1,6]{1,0:T(1,128)} %param.19) | copy-start | bytes 76
  109.5 12.7 %copy-start.7 = (u32[256]{0:T(256)S(1)}, u32[256]{0:T(256)}, u32[]{:S(2)}) copy-start(u32[256]{0:T(256)} %constant.128) | copy-start | bytes 3076
  109.5 13.9 %copy-start.6 = (s32[1,32]{1,0:T(1,128)S(1)}, s32[1,32]{1,0:T(1,128)}, u32[]{:S(2)}) copy-start(s32[1,32]{1,0:T(1,128)} %param.18) | copy-start | bytes 388
  181.9 1.2 copy-start.4
  183.1 16.9 %collective-permute-start.1 = (bf16[1024,2,288]{0,2,1:T(8,128)(2,1)}, bf16[1024,2,288]{0,2,1:T(8,128)(2,1)S(1)}, u32[]{:S(2)}, u32[]{:S(2)}) collective-permute-start(bf16[1024,2,288]{0,2,1:T(8,128)(2,1)} %pad_maximum_fusion.1), channel_id=1, source_target_pairs={{0,2},{1,3},{2,0},{3,1},{4,6},{5,7},{6,4},{7,5},{8,10},{9,11},{10,... | collective-permute-start | bytes 3538952 | tf_op jit(solution)/shard_map/ppermute | solution.py:16
  303.9 56.2 %collective-permute-start.3 = (f32[1024,3,4,32]{0,3,2,1:T(8,128)S(1)}, f32[1024,3,4,32]{0,3,2,1:T(8,128)S(1)}, u32[]{:S(2)}, u32[]{:S(2)}) collective-permute-start(f32[1024,3,4,32]{0,3,2,1:T(8,128)S(1)} %reshape.154), channel_id=1, source_target_pairs={{0,1},{1,0},{2,3},{3,2},{4,5},{5,4},{6,7},{7,6},{8,9},{9,8},{10,11... | collective-permute-start | bytes 4718600 | tf_op jit(solution)/shard_map/ppermute | solution.py:16
  304.7 57.2 %collective-permute-start.9 = (f32[1024,3,4,32]{0,3,2,1:T(8,128)S(1)}, f32[1024,3,4,32]{0,3,2,1:T(8,128)S(1)}, u32[]{:S(2)}, u32[]{:S(2)}) collective-permute-start(f32[1024,3,4,32]{0,3,2,1:T(8,128)S(1)} %bitcast.125), channel_id=1, source_target_pairs={{0,1},{1,0},{2,3},{3,2},{4,5},{5,4},{6,7},{7,6},{8,9},{9,8},{10,11... | collective-permute-start | bytes 4718600 | tf_op jit(solution)/shard_map/ppermute | solution.py:16
  306.2 50.7 %collective-permute-start.2 = (f32[1024,3]{0,1:T(4,128)S(1)}, f32[1024,3]{0,1:T(4,128)S(1)}, u32[]{:S(2)}, u32[]{:S(2)}) collective-permute-start(f32[1024,3]{0,1:T(4,128)S(1)} %bitcast.134), channel_id=1, source_target_pairs={{0,1},{1,0},{2,3},{3,2},{4,5},{5,4},{6,7},{7,6},{8,9},{9,8},{10,11... | collective-permute-start | bytes 36872 | tf_op jit(solution)/shard_map/ppermute | solution.py:16
  306.6 50.7 %collective-permute-start.6 = (f32[1024,3]{0,1:T(4,128)S(1)}, f32[1024,3]{0,1:T(4,128)S(1)}, u32[]{:S(2)}, u32[]{:S(2)}) collective-permute-start(f32[1024,3]{0,1:T(4,128)S(1)} %bitcast.136), channel_id=1, source_target_pairs={{0,1},{1,0},{2,3},{3,2},{4,5},{5,4},{6,7},{7,6},{8,9},{9,8},{10,11... | collective-permute-start | bytes 36872 | tf_op jit(solution)/shard_map/ppermute | solution.py:16
  307.9 52.2 %collective-permute-start.8 = (f32[1024,3]{0,1:T(4,128)S(1)}, f32[1024,3]{0,1:T(4,128)S(1)}, u32[]{:S(2)}, u32[]{:S(2)}) collective-permute-start(f32[1024,3]{0,1:T(4,128)S(1)} %get-tuple-element.107), channel_id=1, source_target_pairs={{0,1},{1,0},{2,3},{3,2},{4,5},{5,4},{6,7},{7,6},{8,9},{9,8},{10,11... | collective-permute-start | bytes 36872 | tf_op jit(solution)/shard_map/ppermute | solution.py:16
  357.0 3.1 collective-permute-start.12
  361.6 65.0 %collective-permute-start.5 = (f32[1024,3,4,32]{0,3,2,1:T(8,128)}, f32[1024,3,4,32]{0,3,2,1:T(8,128)}, u32[]{:S(2)}, u32[]{:S(2)}) collective-permute-start(f32[1024,3,4,32]{0,3,2,1:T(8,128)} %multiply_add_fusion.1), channel_id=1, source_target_pairs={{0,2},{1,3},{2,0},{3,1},{4,6},{5,7},{6,4},{7,5},{8,10},{9,11},{10,... | collective-permute-start | bytes 4718600 | tf_op jit(solution)/shard_map/ppermute | solution.py:16
  362.2 65.8 %copy-start.3 = (bf16[1,96,3072]{2,1,0:T(8,128)(2,1)S(1)}, bf16[1,96,3072]{2,1,0:T(8,128)(2,1)}, u32[]{:S(2)}) copy-start(bf16[1,96,3072]{2,1,0:T(8,128)(2,1)} %param.15) | copy-start | bytes 1769476
  362.2 64.4 %collective-permute-start.11 = (f32[1024,3,4,32]{0,3,2,1:T(8,128)S(1)}, f32[1024,3,4,32]{0,3,2,1:T(8,128)}, u32[]{:S(2)}, u32[]{:S(2)}) collective-permute-start(f32[1024,3,4,32]{0,3,2,1:T(8,128)S(1)} %multiply_add_fusion), channel_id=1, source_target_pairs={{0,2},{1,3},{2,0},{3,1},{4,6},{5,7},{6,4},{7,5},{8,10},{9,11},{10,... | collective-permute-start | bytes 4718600 | tf_op jit(solution)/shard_map/ppermute | solution.py:16
  365.0 56.0 %collective-permute-start.4 = (f32[1024,3]{0,1:T(4,128)S(1)}, f32[1024,3]{0,1:T(4,128)S(1)}, u32[]{:S(2)}, u32[]{:S(2)}) collective-permute-start(f32[1024,3]{0,1:T(4,128)S(1)} %get-tuple-element.83), channel_id=1, source_target_pairs={{0,2},{1,3},{2,0},{3,1},{4,6},{5,7},{6,4},{7,5},{8,10},{9,11},{10,... | collective-permute-start | bytes 36872 | tf_op jit(solution)/shard_map/ppermute | solution.py:16
  365.3 59.5 %collective-permute-start.7 = (f32[1024,3]{0,1:T(4,128)S(1)}, f32[1024,3]{0,1:T(4,128)S(1)}, u32[]{:S(2)}, u32[]{:S(2)}) collective-permute-start(f32[1024,3]{0,1:T(4,128)S(1)} %get-tuple-element.80), channel_id=1, source_target_pairs={{0,2},{1,3},{2,0},{3,1},{4,6},{5,7},{6,4},{7,5},{8,10},{9,11},{10,... | collective-permute-start | bytes 36872 | tf_op jit(solution)/shard_map/ppermute | solution.py:16
  368.0 56.8 %collective-permute-start.10 = (f32[1024,3]{0,1:T(4,128)S(1)}, f32[1024,3]{0,1:T(4,128)S(1)}, u32[]{:S(2)}, u32[]{:S(2)}) collective-permute-start(f32[1024,3]{0,1:T(4,128)S(1)} %get-tuple-element.90), channel_id=1, source_target_pairs={{0,2},{1,3},{2,0},{3,1},{4,6},{5,7},{6,4},{7,5},{8,10},{9,11},{10,... | collective-permute-start | bytes 36872 | tf_op jit(solution)/shard_map/ppermute | solution.py:16
  421.0 5.6 collective-permute-start.13
  432.5 251.8 %copy-start.1 = (bf16[1,3072,288]{1,2,0:T(8,128)(2,1)S(1)}, bf16[1,3072,288]{1,2,0:T(8,128)(2,1)}, u32[]{:S(2)}) copy-start(bf16[1,3072,288]{1,2,0:T(8,128)(2,1)} %param.14) | copy-start | bytes 5308420
  432.5 241.8 %copy-start.2 = (bf16[1,32,3072]{2,1,0:T(8,128)(2,1)S(1)}, bf16[1,32,3072]{2,1,0:T(8,128)(2,1)}, u32[]{:S(2)}) copy-start(bf16[1,32,3072]{2,1,0:T(8,128)(2,1)} %param.11) | copy-start | bytes 589828
  675.3 8.4 %collective-permute-start.14 = (bf16[1,32,3072]{2,1,0:T(8,128)(2,1)S(1)}, bf16[1,32,3072]{2,1,0:T(8,128)(2,1)S(1)}, u32[]{:S(2)}, u32[]{:S(2)}) collective-permute-start(bf16[1,32,3072]{2,1,0:T(8,128)(2,1)S(1)} %fusion.47), channel_id=1, source_target_pairs={{0,32},{32,64},{64,96},{96,128},{128,160},{160,192},{192,224},{224... | collective-permute-start | bytes 589832 | tf_op jit(solution)/shard_map/ppermute | solution.py:21
Sparse Core Ops, SparseCore 0:
  11.6 92.1 all-gather.2
  432.6 241.5 reduce-scatter.1
where the time goes:
time: 694 us; the launch traced here: 691 us
  waiting for transfers between devices  454 us (65%)
  local copies, waits for them, and re-layouts  63.5 us (9%)
  blocking collectives  58.1 us (8%)
  matrix products  46.9 us (7%)
  other arithmetic  33.5 us (5%)
  starting transfers between devices  19.8 us (3%)
  between operations  15.1 us (2%)
    reduce_scatter x1, waiting for transfers between devices, shards(): lax.psum_scatter(jnp.dot(mixed, proj_weight, preferred_element_type=jnp.f...  242 us
    ppermute x14, waiting for transfers between devices, from_partner(): lax.ppermute(x, axis, [(i, i ^ 1 << apart) for i in range(lax.axis_size(a...  117 us
    all_gather x1, waiting for transfers between devices, shards(): lax.all_gather(hidden, 'ulys', axis=0, tiled=True)  92.3 us
    unnamed x1, blocking collectives  58.1 us
    dynamic_update_slice x6, local copies, waits for them, and re-layouts, shards(): lax.map(attend_rows, queries.reshape(block_count, query_block, HPD, HD))  31.1 us
    dot_general x3, matrix products, block_attend(): jnp.einsum('qhd,khd->qhk', queries, keys, preferred_element_type=jnp.floa...  19.3 us
    reduce_sum x3, other arithmetic, block_attend(): total = jnp.sum(weights, axis=2)  19.3 us
    dot_general x3, matrix products, block_attend(): jnp.einsum('qhk,khd->qhd', weights.astype(jnp.bfloat16), values, preferre...  18.3 us
  transfers between devices with their start and end apart: 17, of which 9 were waited for; matrix products, arithmetic and copies ran while one was open for 3% of the time, Pallas kernels for 0%

commit v1 on v0

v1 whole, which is shorter than its diff:
```python
import functools

import jax
import jax.numpy as jnp
from jax import lax
from jax.experimental import pallas as pl
from jax.experimental.pallas import tpu as pltpu
from jax.sharding import PartitionSpec as P

MESH = pl.DeviceIdType.MESH
HD = 128
HPD = 3
NZ = 8
NY = 4
SUBJ = 6
NEG_BIG = -1e30
FACTOR = HD**-0.5
LOG2E = 1.4426950408889634
SCALE = FACTOR * LOG2E
F32 = jnp.float32
BF16 = jnp.bfloat16


def iota(shape, dim):
    return lax.broadcasted_iota(jnp.int32, shape, dim)


def one_hot(cond):
    return jnp.where(cond, 1.0, 0.0).astype(BF16)


def dot_nt(a, b):
    return lax.dot_general(a, b, (((1,), (1,)), ((), ())), preferred_element_type=F32)


def dot(a, b):
    return jnp.dot(a, b, preferred_element_type=F32)


def kernel(
    act, modul, patch, wt, wo, cache, ids, region, counts,
    out,
    hid, wts, cbuf, keys, vals, pieces, qx, kvx, queries, fresh_k, fresh_v,
    po_send, po, ml_send, ml, gk, woall, part, rs_send, rs_recv, reg, res, place,
    own_sem, hid_ss, hid_rs, q_ss, q_rs, kv_ss, kv_rs, po_ss, po_rs, ml_ss, ml_rs,
    gk_ss, gk_rs, wo_ss, wo_rs, rs_ss, rs_rs, reg_ss, reg_rs, res_ss, res_rs, c_sem, w_sem,
):
    pipe = lax.axis_index("pipe")
    u = lax.axis_index("ulys")
    z, y = u // NY, lax.rem(u, NY)
    rows, width = act.shape
    line = NZ * rows
    half = width // 2
    span = cache.shape[0]
    chunk = span // 3

    def at_y(j):
        return lax.rem(y + j, NY)

    def at_z(k):
        return lax.rem(z + k + NZ, NZ)

    def dev(zz, yy):
        return (pipe, zz * NY + yy)

    after, before = lax.rem(pipe + 1, 8), lax.rem(pipe + 7, 8)

    def remote(src, dst, ss, rs, target):
        return pltpu.make_async_remote_copy(src, dst, ss, rs, target, device_id_type=MESH)

    block = wt.shape[0] // 3
    w_copies = [
        pltpu.make_async_copy(wt.at[pl.ds(i * block, block)], wts.at[pl.ds(i * 128, block)], w_sem.at[i])
        for i in range(3)
    ]
    for copy in w_copies:
        copy.start()

    def cache_copy(i):
        return pltpu.make_async_copy(cache.at[pl.ds(i * 256, 256)], cbuf.at[lax.rem(i, 2)], c_sem.at[lax.rem(i, 2)])

    cache_copy(0).start()

    barrier = pltpu.get_barrier_semaphore()
    greeted = [dev(z, at_y(j)) for j in range(1, NY)] + [dev(at_z(k), y) for k in range(1, NZ)]
    greeted += [(after, u), (before, u)]
    for target in greeted:
        pl.semaphore_signal(barrier, inc=1, device_id=target, device_id_type=MESH)

    lifted = act[...].astype(F32)
    center = jnp.mean(lifted, axis=1, keepdims=True)
    spread = jnp.mean(jnp.square(lifted - center), axis=1, keepdims=True)
    normed = (lifted - center) * lax.rsqrt(spread + 1e-06)
    hid[y, z] = (normed * (1.0 + modul[1]) + modul[0]).astype(BF16)
    diagonal = iota((rows, rows), 0) == iota((rows, rows), 1)
    wide = jnp.broadcast_to(region[...].astype(F32), (rows, rows))
    column = jnp.sum(jnp.where(diagonal, wide, 0.0), axis=1, keepdims=True)
    reg[z] = jnp.broadcast_to(column, (rows, 128))

    slots = ids.shape[0]
    packed = ids[...].reshape(2 * slots, HPD * HD)
    pick = iota((slots, 2 * slots), 1) - 2 * iota((slots, 2 * slots), 0)
    gk[y, :, 0 : HPD * HD] = dot(one_hot(pick == 0), packed).astype(BF16)
    gk[y, :, HPD * HD :] = dot(one_hot(pick == 1), packed).astype(BF16)

    pl.semaphore_wait(barrier, len(greeted))

    sends = []

    def go(copy):
        copy.start()
        sends.append(copy)

    def send_hid(yy, zz, slot, target):
        go(remote(hid.at[yy, zz], hid.at[yy, zz], hid_ss.at[slot], hid_rs.at[yy, zz], target))

    def wait_hid(yy, zz):
        remote(hid.at[yy, zz], hid.at[yy, zz], hid_ss.at[0], hid_rs.at[yy, zz], dev(z, y)).wait_recv()

    slot = iter(range(64))
    up, down = dev(at_z(1), y), dev(at_z(-1), y)
    left, right, far = dev(z, at_y(3)), dev(z, at_y(1)), dev(z, at_y(2))
    for target in (up, down, left, right, far):
        send_hid(y, z, next(slot), target)
    for k in range(1, NZ):
        go(remote(reg.at[z], reg.at[z], reg_ss.at[k - 1], reg_rs.at[z], dev(at_z(k), y)))
    for j in range(1, NY):
        go(remote(gk.at[y], gk.at[y], gk_ss.at[j - 1], gk_rs.at[y], dev(z, at_y(j))))

    spot, goal = iota((NY * 128, HPD * HD), 0), iota((NY * 128, HPD * HD), 1)
    inner = lax.rem(spot, 128)
    found = (spot // 128 == lax.rem(goal, 128) // 32) & (inner // 32 == goal // 128)
    place[...] = one_hot(found & (lax.rem(inner, 32) == lax.rem(goal, 32)))
    for i in range(3):
        wts[pl.ds(i * 128 + block, 128 - block)] = jnp.zeros((128 - block, width), BF16)

    pick_c = iota((256, 512), 1) - 2 * iota((256, 512), 0)
    even, odd = one_hot(pick_c == 0), one_hot(pick_c == 1)

    def split_cache(i, last):
        if not last:
            cache_copy(i + 1).start()
        cache_copy(i).wait()
        x = cbuf[lax.rem(i, 2)].reshape(512, HPD * HD)
        kk = dot(even, x).astype(BF16)
        vv = dot(odd, x).astype(BF16)
        for h in range(HPD):
            keys[h, pl.ds(pl.multiple_of(i * 256, 256), 256)] = kk[:, h * HD : (h + 1) * HD]
            vals[h, pl.ds(pl.multiple_of(i * 256, 256), 256)] = vv[:, h * HD : (h + 1) * HD]

    def split_some(first, count, last=False):
        def body(i, _):
            split_cache(first + i, False)
            return 0

        lax.fori_loop(0, count - (1 if last else 0), body, 0)
        if last:
            split_cache(jnp.int32(first + count - 1), True)

    split_some(0, 4)

    opposite = at_y(2)
    wait_hid(opposite, z)
    send_hid(opposite, z, next(slot), up)
    send_hid(opposite, z, next(slot), down)
    for k in range(1, 5):
        wait_hid(y, at_z(-k))
        if k < 4:
            send_hid(y, at_z(-k), next(slot), up)
        send_hid(y, at_z(-k), next(slot), left)
        send_hid(y, at_z(-k), next(slot), right)
        if k < 4:
            wait_hid(y, at_z(k))
            if k < 3:
                send_hid(y, at_z(k), next(slot), down)
            send_hid(y, at_z(k), next(slot), left)
            send_hid(y, at_z(k), next(slot), right)
        wait_hid(opposite, at_z(k))
        if k < 4:
            send_hid(opposite, at_z(k), next(slot), down)
        if k < 4:
            wait_hid(opposite, at_z(-k))
            if k < 3:
                send_hid(opposite, at_z(-k), next(slot), up)
        split_some(4 + 2 * (k - 1), 2, k == 4)
    for copy in w_copies:
        copy.wait()

    def project(i, _):
        ln = at_y(i)

        @pl.when(lax.rem(i, 2) == 1)
        def _():
            def body(zz, _):
                wait_hid(ln, zz)
                return 0

            lax.fori_loop(0, NZ, body, 0)

        base = pl.multiple_of(ln * line, line)
        x = hid[ln].reshape(line, width)
        pieces[pl.ds(base, line)] = dot_nt(x, wts[...]).astype(BF16)
        qx[y, pl.ds(base, line)] = pieces[pl.ds(base, line), 0:128]

        def send_q(j, _):
            s = pieces.at[pl.ds(base, line), pl.ds(0, 128)]
            d = qx.at[y, pl.ds(base, line)]
            remote(s, d, q_ss.at[j, ln], q_rs.at[y, ln], dev(z, at_y(j))).start()
            return 0

        lax.fori_loop(1, NY, send_q, 0)

        @pl.when(i != 0)
        def _():
            s = pieces.at[pl.ds(base, line), pl.ds(128, 256)]
            remote(s, kvx.at[y], kv_ss.at[i], kv_rs.at[y], dev(z, ln)).start()

        @pl.when(i == 0)
        def _():
            kvx[y] = pieces[pl.ds(base, line), 128:384]

        return 0

    lax.fori_loop(0, NY, project, 0)

    own_wo = pltpu.make_async_copy(wo, woall.at[y], own_sem)
    own_wo.start()
    for j in range(1, NY):
        go(remote(wo, woall.at[y], wo_ss.at[j - 1], wo_rs.at[y], dev(z, at_y(j))))

    def line_ref(ref, ln):
        return ref.at[pl.ds(pl.multiple_of(ln * line, line), line)]

    def recv(ref, rs):
        remote(ref, ref, hid_ss.at[0], rs, dev(z, y)).wait_recv()

    for j in range(1, NY):
        recv(kvx.at[at_y(j)], kv_rs.at[at_y(j)])
    both = [
        sum(dot(kvx[yy, :, s * 128 : s * 128 + 128], place[yy * 128 : yy * 128 + 128]) for yy in range(NY)).astype(BF16)
        for s in range(2)
    ]
    for h in range(HPD):
        fresh_k[h] = both[0][:, h * HD : (h + 1) * HD]
        fresh_v[h] = both[1][:, h * HD : (h + 1) * HD]

    lane = iota((line, 128), 1)

    def attend_head(ln, h, packed_ml):
        q = queries[h, pl.ds(pl.multiple_of(ln * line, line), line)]
        peaks, totals, outs = [], [], []
        for c in range(4):
            if c < 3:
                kk, vv = keys[h, c * chunk : (c + 1) * chunk], vals[h, c * chunk : (c + 1) * chunk]
            else:
                kk, vv = fresh_k[h], fresh_v[h]
            s = dot_nt(q, kk)
            peak = jnp.max(s, axis=1, keepdims=True)
            w = jnp.exp2((s - peak) * SCALE)
            totals.append(jnp.sum(w, axis=1, keepdims=True))
            outs.append(dot(w.astype(BF16), vv))
            if c < 3:
                stale = patch[0] == y * 3 + c
                peak = jnp.where(stale, NEG_BIG, peak)
            peaks.append(peak)
        peak = jnp.maximum(jnp.maximum(peaks[0], peaks[1]), jnp.maximum(peaks[2], peaks[3]))
        alphas = [jnp.exp2((p - peak) * SCALE) for p in peaks]
        total = sum(a * t for a, t in zip(alphas, totals))
        own = sum(a * o for a, o in zip(alphas, outs))
        packed_ml = jnp.where(lane == h, peak, packed_ml)
        packed_ml = jnp.where(lane == h + HPD, total, packed_ml)
        return own / total, packed_ml

    def attend_line(i, _):
        ln = at_y(i + 1)
        base = pl.multiple_of(ln * line, line)
        for j in range(1, NY):
            yy = at_y(j)
            recv(qx.at[yy, pl.ds(base, line)], q_rs.at[yy, ln])
        full = sum(dot(qx[yy, pl.ds(base, line)], place[yy * 128 : yy * 128 + 128]) for yy in range(NY)).astype(BF16)
        for h in range(HPD):
            queries[h, pl.ds(base, line)] = full[:, h * HD : (h + 1) * HD]

        def head(h, packed_ml):
            normal, packed_ml = attend_head(ln, h, packed_ml)
            po_send[ln, h] = normal.astype(BF16)
            return packed_ml

        packed_ml = lax.fori_loop(0, HPD, head, jnp.zeros((line, 128), F32))
        ml_send[ln] = jnp.transpose(packed_ml)[0:8]

        @pl.when(i < NY - 1)
        def _():
            target = dev(z, ln)
            remote(po_send.at[ln], po.at[y], po_ss.at[ln], po_rs.at[y], target).start()
            remote(ml_send.at[ln], ml.at[y], ml_ss.at[ln], ml_rs.at[y], target).start()

        return 0

    lax.fori_loop(0, NY, attend_line, 0)
    po[y] = po_send[y]
    ml[y] = ml_send[y]

    def recv_reg(k, _):
        zz = at_z(k)
        recv(reg.at[zz], reg_rs.at[zz])
        return 0

    lax.fori_loop(1, NZ, recv_reg, 0)
    for j in range(1, NY):
        recv(gk.at[at_y(j)], gk_rs.at[at_y(j)])
    total_slots = NY * slots
    per_subject = slots // SUBJ
    spot = iota((line, total_slots), 1)
    inside = lax.rem(spot, slots)
    subject = inside // per_subject
    slot_index = spot // slots * per_subject + lax.rem(inside, per_subject)
    live = jnp.zeros((line, total_slots), jnp.int32)
    for s in range(SUBJ):
        live = jnp.where(subject == s, counts[0, s], live)
    regions = reg[...].reshape(line, 128)[:, 0:1]
    mask = (regions == (subject + 1).astype(F32)) & (slot_index < live)
    own_base = pl.multiple_of(y * line, line)
    guests = []
    for h in range(HPD):
        q = queries[h, pl.ds(own_base, line)]
        g_keys = gk[:, :, h * HD : (h + 1) * HD].reshape(total_slots, HD)
        g_vals = gk[:, :, (HPD + h) * HD : (HPD + h + 1) * HD].reshape(total_slots, HD)
        s = dot_nt(q, g_keys)
        peak = jnp.max(jnp.where(mask, s, NEG_BIG), axis=1, keepdims=True)
        w = jnp.where(mask, jnp.exp2(jnp.where(mask, (s - peak) * SCALE, 0.0)), 0.0)
        total = jnp.maximum(jnp.sum(w, axis=1, keepdims=True), 1.0)
        guests.append(dot(w.astype(BF16), g_vals) / total)

    for j in range(1, NY):
        recv(po.at[at_y(j)], po_rs.at[at_y(j)])
        recv(ml.at[at_y(j)], ml_rs.at[at_y(j)])
    stats = jnp.concatenate([ml[...].reshape(NY * 8, line), jnp.zeros((128 - NY * 8, line), F32)], axis=0)
    stats = jnp.transpose(stats)
    mixed = []
    for h in range(HPD):
        peaks = [stats[:, yy * 8 + h : yy * 8 + h + 1] for yy in range(NY)]
        totals = [stats[:, yy * 8 + HPD + h : yy * 8 + HPD + h + 1] for yy in range(NY)]
        peak = jnp.maximum(jnp.maximum(peaks[0], peaks[1]), jnp.maximum(peaks[2], peaks[3]))
        shares = [jnp.exp2((p - peak) * SCALE) * t for p, t in zip(peaks, totals)]
        whole = shares[0] + shares[1] + shares[2] + shares[3]
        own = sum(po[yy, h].astype(F32) * (shares[yy] / whole) for yy in range(NY))
        mixed.append((own + guests[h]).astype(BF16))

    own_wo.wait()
    for j in range(1, NY):
        recv(woall.at[at_y(j)], wo_rs.at[at_y(j)])
    spot, goal = iota((HD, NY * block), 0), iota((HD, NY * block), 1)
    ordered = sum(
        dot(
            mixed[h],
            one_hot(
                (lax.rem(goal, block) // 32 == h) & (goal // block == spot // 32) & (lax.rem(goal, 32) == lax.rem(spot, 32))
            ),
        )
        for h in range(HPD)
    ).astype(BF16)
    tile = 512

    def project_out(t, _):
        cols = pl.ds(pl.multiple_of(t * tile, tile), tile)
        w = woall[:, :, cols].reshape(NY * block, tile)
        part[:, :, cols] = dot(ordered, w).reshape(NZ, rows, tile)
        return 0

    lax.fori_loop(0, width // tile, project_out, 0)

    cols = (pl.ds(0, half), pl.ds(half, half))
    for t in range(4):
        for d in range(2):
            for s in range(2):
                hops = 4 if d == s else 3
                if t >= hops:
                    continue
                step = 1 if d == 0 else -1
                term = part[at_z(step * (hops - t)), :, cols[s]]
                if t > 0:
                    recv(rs_recv.at[d, s, t - 1], rs_rs.at[d, s, t - 1])
                    term = term + rs_recv[d, s, t - 1].astype(F32)
                rs_send[d, s, t] = term.astype(BF16)
                go(remote(rs_send.at[d, s, t], rs_recv.at[d, s, t], rs_ss.at[d, s, t], rs_rs.at[d, s, t], dev(at_z(step), y)))
    for s in range(2):
        total = part[z, :, cols[s]]
        for d in range(2):
            last = (4 if d == s else 3) - 1
            recv(rs_recv.at[d, s, last], rs_rs.at[d, s, last])
            total = total + rs_recv[d, s, last].astype(F32)
        gate = modul[2, :, cols[s]]
        res[s] = (act[:, cols[s]].astype(F32) + gate * total).astype(BF16)
        go(remote(res.at[s], out.at[:, cols[s]], res_ss.at[s], res_rs.at[s], (after, u)))
    for s in range(2):
        recv(out.at[:, cols[s]], res_rs.at[s])

    for copy in sends:
        copy.wait_send()

    def drain(i, _):
        ln = at_y(i)
        base = pl.multiple_of(ln * line, line)

        def drain_q(j, _):
            s = pieces.at[pl.ds(base, line), pl.ds(0, 128)]
            remote(s, qx.at[y, pl.ds(base, line)], q_ss.at[j, ln], q_rs.at[y, ln], dev(z, at_y(j))).wait_send()
            return 0

        lax.fori_loop(1, NY, drain_q, 0)

        @pl.when(i != 0)
        def _():
            s = pieces.at[pl.ds(base, line), pl.ds(128, 256)]
            remote(s, kvx.at[y], kv_ss.at[i], kv_rs.at[y], dev(z, ln)).wait_send()
            remote(po_send.at[ln], po.at[y], po_ss.at[ln], po_rs.at[y], dev(z, ln)).wait_send()
            remote(ml_send.at[ln], ml.at[y], ml_ss.at[ln], ml_rs.at[y], dev(z, ln)).wait_send()

        return 0

    lax.fori_loop(0, NY, drain, 0)


def shards(
    activations, patch_index, modulation, qkv_weight, out_weight, stale_cache, id_cache, region_ids, id_counts
):
    _, rows, width = activations.shape
    span = stale_cache.shape[2]
    slots = id_cache.shape[2] * id_cache.shape[3]
    line = NZ * rows
    tokens = NY * line
    block = qkv_weight.shape[2] // 3
    half = width // 2
    dma = pltpu.SemaphoreType.DMA
    vmem = pl.BlockSpec(memory_space=pltpu.VMEM)
    smem = pl.BlockSpec(memory_space=pltpu.SMEM)
    anywhere = pl.BlockSpec(memory_space=pl.ANY)
    result = pl.pallas_call(
        kernel,
        out_shape=jax.ShapeDtypeStruct((rows, width), BF16),
        in_specs=[vmem, vmem, smem, anywhere, anywhere, anywhere, vmem, vmem, smem],
        out_specs=vmem,
        scratch_shapes=[
            pltpu.VMEM((NY, NZ, rows, width), BF16),
            pltpu.VMEM((3 * 128, width), BF16),
            pltpu.VMEM((2, 256, 2, HPD * HD), BF16),
            pltpu.VMEM((HPD, span, HD), BF16),
            pltpu.VMEM((HPD, span, HD), BF16),
            pltpu.VMEM((tokens, 3 * 128), BF16),
            pltpu.VMEM((NY, tokens, 128), BF16),
            pltpu.VMEM((NY, line, 256), BF16),
            pltpu.VMEM((HPD, tokens, HD), BF16),
            pltpu.VMEM((HPD, line, HD), BF16),
            pltpu.VMEM((HPD, line, HD), BF16),
            pltpu.VMEM((NY, HPD, line, HD), BF16),
            pltpu.VMEM((NY, HPD, line, HD), BF16),
            pltpu.VMEM((NY, 8, line), F32),
            pltpu.VMEM((NY, 8, line), F32),
            pltpu.VMEM((NY, slots, 2 * HPD * HD), BF16),
            pltpu.VMEM((NY, block, width), BF16),
            pltpu.VMEM((NZ, rows, width), F32),
            pltpu.VMEM((2, 2, 4, rows, half), BF16),
            pltpu.VMEM((2, 2, 4, rows, half), BF16),
            pltpu.VMEM((NZ, rows, 128), F32),
            pltpu.VMEM((2, rows, half), BF16),
            pltpu.VMEM((NY * 128, HPD * HD), BF16),
            dma,
            dma((64,)), dma((NY, NZ)),
            dma((NY, NY)), dma((NY, NY)),
            dma((NY,)), dma((NY,)),
            dma((NY,)), dma((NY,)),
            dma((NY,)), dma((NY,)),
            dma((NY,)), dma((NY,)),
            dma((NY,)), dma((NY,)),
            dma((2, 2, 4)), dma((2, 2, 4)),
            dma((NZ,)), dma((NZ,)),
            dma((2,)), dma((2,)),
            dma((2,)),
            dma((3,)),
        ],
        compiler_params=pltpu.CompilerParams(
            collective_id=0, has_side_effects=True, vmem_limit_bytes=56 * 2**20
        ),
        name="section",
    )(
        activations[0],
        jnp.transpose(modulation, (1, 0, 2)),
        patch_index,
        jnp.swapaxes(qkv_weight[0], 0, 1),
        out_weight[0],
        stale_cache[0, 0],
        id_cache[0, 0].reshape(slots, 2, HPD * HD),
        region_ids,
        id_counts,
    )
    return result[None]


def solution(mesh):
    placed = (
        P("pipe", "ulys", None),
        P("pipe"),
        P("pipe", None, None),
        P("pipe", None, "ulys"),
        P("pipe", "ulys", None),
        P("pipe", "ulys", None, None, None),
        P("pipe", "ulys", None, None, None, None),
        P("pipe", "ulys"),
        P("pipe", None),
    )
    return jax.shard_map(
        shards, mesh=mesh, in_specs=placed, out_specs=P("pipe", "ulys", None), check_vma=False
    )
```

time: 694 us -> 137 us (0.20)
  the two profiles are of different devices: /device:TPU:1 before, /device:TPU:31 now
where the time goes in v1:
time: 137 us
  Pallas kernels  135 us (99%)
  local copies, waits for them, and re-layouts  1.62 us (1%)
    pallas_call x1, Pallas kernels, shards(): pl.pallas_call(kernel, out_shape=jax.ShapeDtypeStruct((rows, width), BF16...  135 us

profile of v1, /device:TPU:31, one launch (start us, length us, event | category | flops | bytes accessed | tf_op | source)
XLA Modules:
  0.0 136.9 jit_solution(7468524904786548028)
XLA Ops:
  0.7 134.6 %section.1 = bf16[32,3072]{1,0:T(8,128)(2,1)} custom-call(bf16[32,3072]{1,0:T(8,128)(2,1)} %bitcast.13, f32[3,1,3072]{2,1,0:T(1,128)} %bitcast.15, s32[1]{0:T(128)S(6)} %copy.11.patch, bf16[288,3072]{1,0:T(8,128)(2,1)} %bitcast.10, bf16[96,3072]{1,0:T(8,128)(2,1)} %bitcast.12, bf16[3072,2,384]{2,1,0:T(2,128)(2,1)} %bitcast.9, bf16[48,2,384]{2,1,0:T(2,128)(2,1)} %bitcast.14, ...), custom_call_target="tpu_custom_call" | custom-call | tf_op jit(solution)/shard_map/section/pallas_call | solution.py:439
  135.2 1.6 %copy.12 = bf16[1,32,3072]{2,1,0:T(8,128)(2,1)} copy(bf16[1,32,3072]{2,1,0:T(8,128)(2,1)} %bitcast.11) | data formatting | bytes 393216

commit v2 on v1

v2 whole, which is shorter than its diff:
```python
import functools

import jax
import jax.numpy as jnp
from jax import lax
from jax.experimental import pallas as pl
from jax.experimental.pallas import tpu as pltpu
from jax.sharding import PartitionSpec as P

MESH = pl.DeviceIdType.MESH
HD = 128
HPD = 3
NZ = 8
NY = 4
SUBJ = 6
NEG_BIG = -1e30
FACTOR = HD**-0.5
LOG2E = 1.4426950408889634
SCALE = FACTOR * LOG2E
F32 = jnp.float32
BF16 = jnp.bfloat16


def iota(shape, dim):
    return lax.broadcasted_iota(jnp.int32, shape, dim)


def one_hot(cond):
    return jnp.where(cond, 1.0, 0.0).astype(BF16)


def dot_nt(a, b):
    return lax.dot_general(a, b, (((1,), (1,)), ((), ())), preferred_element_type=F32)


def dot(a, b):
    return jnp.dot(a, b, preferred_element_type=F32)


ORDER = (0, -1, 1, -2, 2, -3, 3, 4)
SLOT = {d: i for i, d in enumerate(ORDER)}
SLOT[-4] = SLOT[4]
GROUPS = ((0, 1), (1, 3), (3, 5), (5, 7), (7, 8))


def kernel(
    act, modul, patch, wt, wo, cache, ids, region, counts,
    out,
    hid, wts, cbuf, keys, vals, pieces, qx, kvx, queries, fresh_k, fresh_v, acc, top, mass,
    po_send, po, ml_send, ml, stats, guest, gk, woall, part, rs_send, rs_recv, res, place, reorder,
    hid_ss, hid_rs, q_ss, q_rs, kv_ss, kv_rs, po_ss, po_rs, ml_ss, ml_rs,
    gk_ss, gk_rs, wo_ss, wo_rs, own_sem, rs_ss, rs_rs, res_ss, res_rs, c_sem, w_sem,
):
    pipe = lax.axis_index("pipe")
    u = lax.axis_index("ulys")
    z, y = u // NY, lax.rem(u, NY)
    rows, width = act.shape
    quad = NY * rows
    line = NZ * rows
    split = (width * 3 // 4) // 128 * 128
    span = cache.shape[0]
    chunk = span // 3

    def at_y(j):
        return lax.rem(y + j, NY)

    def at_z(k):
        return lax.rem(z + k + NZ, NZ)

    def dev(zz, yy):
        return (pipe, zz * NY + yy)

    after, before = lax.rem(pipe + 1, 8), lax.rem(pipe + 7, 8)
    up, down = dev(at_z(1), y), dev(at_z(-1), y)
    right, far, left = (dev(z, at_y(j)) for j in range(1, NY))
    peers = (right, far, left)

    def remote(src, dst, ss, rs, target):
        return pltpu.make_async_remote_copy(src, dst, ss, rs, target, device_id_type=MESH)

    block = wt.shape[0] // 3
    w_copies = [
        pltpu.make_async_copy(wt.at[pl.ds(i * block, block)], wts.at[pl.ds(i * 128, block)], w_sem.at[i])
        for i in range(3)
    ]
    for copy in w_copies:
        copy.start()

    def cache_copy(i):
        return pltpu.make_async_copy(cache.at[pl.ds(i * 256, 256)], cbuf.at[lax.rem(i, 2)], c_sem.at[lax.rem(i, 2)])

    cache_copy(0).start()
    own_wo = pltpu.make_async_copy(wo, woall.at[y], own_sem)
    own_wo.start()

    barrier = pltpu.get_barrier_semaphore()
    greeted = [right, far, left, up, down, (after, u), (before, u)]
    for target in greeted:
        pl.semaphore_signal(barrier, inc=1, device_id=target, device_id_type=MESH)

    lifted = act[...].astype(F32)
    center = jnp.mean(lifted, axis=1, keepdims=True)
    spread = jnp.mean(jnp.square(lifted - center), axis=1, keepdims=True)
    normed = (lifted - center) * lax.rsqrt(spread + 1e-06)
    hid[0, y, :, 0:width] = (normed * (1.0 + modul[1]) + modul[0]).astype(BF16)
    diagonal = iota((rows, rows), 0) == iota((rows, rows), 1)
    wide = jnp.broadcast_to(region[...].astype(F32), (rows, rows))
    column = jnp.sum(jnp.where(diagonal, wide, 0.0), axis=1, keepdims=True)
    hid[0, y, :, width:] = jnp.broadcast_to(column, (rows, 128)).astype(BF16)

    slots = ids.shape[0]
    packed = ids[...].reshape(2 * slots, HPD * HD)
    pick = iota((slots, 2 * slots), 1) - 2 * iota((slots, 2 * slots), 0)
    gk[y, :, 0 : HPD * HD] = dot(one_hot(pick == 0), packed).astype(BF16)
    gk[y, :, HPD * HD :] = dot(one_hot(pick == 1), packed).astype(BF16)

    pl.semaphore_wait(barrier, len(greeted))

    sends = []

    def go(copy):
        copy.start()
        sends.append(copy)

    def recv(ref, rs):
        remote(ref, ref, hid_ss.at[0], rs, dev(z, y)).wait_recv()

    parts = {
        "r": (pl.ds(0, width + 128), 0),
        "w": (pl.ds(0, width), 0),
        "a": (pl.ds(0, split), 0),
        "b": (pl.ds(width - split, split), 0),
        "c": (pl.ds(0, width - split), 1),
        "d": (pl.ds(split, width - split), 1),
    }
    next_send = iter(range(64))

    def send_hid(d, yy, what, target, d_there):
        cols, n = parts[what]
        src, dst = hid.at[SLOT[d], yy, :, cols], hid.at[SLOT[d_there], yy, :, cols]
        go(remote(src, dst, hid_ss.at[next(next_send)], hid_rs.at[SLOT[d_there], yy, n], target))

    def wait_hid(d, yy, what):
        cols, n = parts[what]
        recv(hid.at[SLOT[d], yy, :, cols], hid_rs.at[SLOT[d], yy, n])

    streams = ((y, "r", 4, 3), (at_y(1), "a", 4, 3), (at_y(3), "b", 3, 4), (at_y(2), "w", 3, 4))

    wo_half = [pl.ds(i * (block // 2), block // 2) for i in range(2)]

    def wait_wo(yy, i):
        recv(woall.at[yy, wo_half[i]], wo_rs.at[yy, i])

    def send_wo(i):
        for j, target in enumerate((right, left)):
            go(remote(wo.at[wo_half[i]], woall.at[y, wo_half[i]], wo_ss.at[j, i], wo_rs.at[y, i], target))

    def pass_wo():
        for i, (yy, target) in enumerate(((at_y(3), right), (at_y(1), left))):
            wait_wo(yy, i)
            ref = woall.at[yy, wo_half[i]]
            go(remote(ref, ref, wo_ss.at[2, i], wo_rs.at[yy, i], target))

    send_hid(0, y, "r", up, -1)
    send_hid(0, y, "r", down, 1)
    for what, target in (("a", left), ("b", right), ("w", far), ("d", left), ("c", right)):
        send_hid(0, y, what, target, 0)

    spot, goal = iota((NY * 128, HPD * HD), 0), iota((NY * 128, HPD * HD), 1)
    inner = lax.rem(spot, 128)
    found = (spot // 128 == lax.rem(goal, 128) // 32) & (inner // 32 == goal // 128)
    place[...] = one_hot(found & (lax.rem(inner, 32) == lax.rem(goal, 32)))
    spot, goal = iota((HPD * HD, NY * block), 0), iota((HPD * HD, NY * block), 1)
    found = (goal // block == lax.rem(spot, HD) // 32) & (lax.rem(goal, block) // 32 == spot // HD)
    reorder[...] = one_hot(found & (lax.rem(goal, 32) == lax.rem(spot, 32)))
    for i in range(3):
        wts[pl.ds(i * 128 + block, 128 - block)] = jnp.zeros((128 - block, width), BF16)

    pick_c = iota((256, 512), 1) - 2 * iota((256, 512), 0)
    even, odd = one_hot(pick_c == 0), one_hot(pick_c == 1)

    def split_cache(i, last):
        if not last:
            cache_copy(i + 1).start()
        cache_copy(i).wait()
        x = cbuf[lax.rem(i, 2)].reshape(512, HPD * HD)
        kk = dot(even, x).astype(BF16)
        vv = dot(odd, x).astype(BF16)
        for h in range(HPD):
            keys[h, pl.ds(pl.multiple_of(i * 256, 256), 256)] = kk[:, h * HD : (h + 1) * HD]
            vals[h, pl.ds(pl.multiple_of(i * 256, 256), 256)] = vv[:, h * HD : (h + 1) * HD]

    def split_some(first, count, last=False):
        def body(i, _):
            split_cache(first + i, False)
            return 0

        lax.fori_loop(0, count - (1 if last else 0), body, 0)
        if last:
            split_cache(jnp.int32(first + count - 1), True)

    def span_of(g):
        first, end = GROUPS[g]
        return first * quad, (end - first) * quad

    def project(g):
        first, end = GROUPS[g]
        for d in ORDER[first:end]:
            wait_hid(d, at_y(3), "c")
            wait_hid(d, at_y(1), "d")
        base, size = span_of(g)
        x = hid[first:end, :, :, 0:width].reshape(size, width)
        p = dot_nt(x, wts[...]).astype(BF16)
        pieces[first:end] = p.reshape(end - first, NY, rows, 3 * 128)
        qx[y, pl.ds(base, size)] = p[:, 0:128]
        for j, target in enumerate(peers):
            q = qx.at[y, pl.ds(base, size)]
            go(remote(q, q, q_ss.at[g, j], q_rs.at[g, y], target))
        for j, target in enumerate(peers):
            kv = pieces.at[pl.ds(first, end - first), at_y(j + 1), :, pl.ds(128, 256)]
            go(remote(kv, kvx.at[y, pl.ds(first, end - first)], kv_ss.at[g, j], kv_rs.at[g, y], target))
        kvx[y, first:end] = pieces[first:end, y, :, 128:384]

    lane = iota((256, 128), 1)

    def place_queries(g):
        base, size = span_of(g)
        for j in range(1, NY):
            recv(qx.at[at_y(j), pl.ds(base, size)], q_rs.at[g, at_y(j)])
        full = sum(dot(qx[yy, pl.ds(base, size)], place[yy * 128 : yy * 128 + 128]) for yy in range(NY)).astype(BF16)
        for h in range(HPD):
            queries[h, pl.ds(base, size)] = full[:, h * HD : (h + 1) * HD]

    def attend_keys(h, base, size, with_fresh):
        q = queries[h, pl.ds(base, size)]
        scores = [dot_nt(q, keys[h, c * chunk : (c + 1) * chunk]) for c in range(3)]
        peaks = [jnp.max(s, axis=1, keepdims=True) for s in scores]
        replaced = [patch[0] == y * 3 + c for c in range(3)]
        peaks = [jnp.where(r, NEG_BIG, p) for r, p in zip(replaced, peaks)]
        peak = jnp.maximum(jnp.maximum(peaks[0], peaks[1]), peaks[2])
        if with_fresh:
            fresh_scores = dot_nt(q, fresh_k[h])
            peak = jnp.maximum(peak, jnp.max(fresh_scores, axis=1, keepdims=True))
        total, own = 0.0, 0.0
        for c in range(3):
            w = jnp.exp2((scores[c] - jnp.where(replaced[c], -NEG_BIG, peak)) * SCALE)
            total = total + jnp.sum(w, axis=1, keepdims=True)
            own = own + dot(w.astype(BF16), vals[h, c * chunk : (c + 1) * chunk])
        if with_fresh:
            w = jnp.exp2((fresh_scores - peak) * SCALE)
            total = total + jnp.sum(w, axis=1, keepdims=True)
            own = own + dot(w.astype(BF16), fresh_v[h])
        return peak, total, own

    def attend(g):
        base, size = span_of(g)
        place_queries(g)

        def head(h, _):
            peak, total, own = attend_keys(h, base, size, False)
            acc[h, pl.ds(base, size)] = own
            top[h, pl.ds(base, size)] = jnp.broadcast_to(peak, (size, 128))
            mass[h, pl.ds(base, size)] = jnp.broadcast_to(total, (size, 128))
            return 0

        lax.fori_loop(0, HPD, head, 0)

    total_slots = NY * slots
    per_subject = slots // SUBJ

    def attend_guests(g):
        first, end = GROUPS[g]
        mine = (end - first) * rows
        spot = iota((mine, total_slots), 1)
        inside = lax.rem(spot, slots)
        subject = inside // per_subject
        slot_index = spot // slots * per_subject + lax.rem(inside, per_subject)
        live = jnp.zeros((mine, total_slots), jnp.int32)
        for s in range(SUBJ):
            live = jnp.where(subject == s, counts[0, s], live)
        regions = hid[first:end, y, :, width:].reshape(mine, 128).astype(F32)[:, 0:1]
        mask = (regions == (subject + 1).astype(F32)) & (slot_index < live)
        for h in range(HPD):
            own_rows = [queries[h, pl.ds(pl.multiple_of(i * quad + y * rows, rows), rows)] for i in range(first, end)]
            q = jnp.concatenate(own_rows, axis=0)
            g_keys = gk[:, :, h * HD : (h + 1) * HD].reshape(total_slots, HD)
            g_vals = gk[:, :, (HPD + h) * HD : (HPD + h + 1) * HD].reshape(total_slots, HD)
            s = dot_nt(q, g_keys)
            peak = jnp.max(jnp.where(mask, s, NEG_BIG), axis=1, keepdims=True)
            w = jnp.where(mask, jnp.exp2(jnp.where(mask, (s - peak) * SCALE, 0.0)), 0.0)
            total = jnp.maximum(jnp.sum(w, axis=1, keepdims=True), 1.0)
            guest[h, first * rows : end * rows] = dot(w.astype(BF16), g_vals) / total

    def send_group(g, packed_ml):
        first, end = GROUPS[g]
        base, size = span_of(g)
        for j, target in enumerate(peers):
            src = po_send.at[pl.ds(first, end - first), at_y(j + 1)]
            go(remote(src, po.at[y, pl.ds(first, end - first)], po_ss.at[g, j], po_rs.at[g, y], target))
        ml_send[:, base : base + size] = jnp.transpose(packed_ml)[0:8]
        for j, target in enumerate(peers):
            src, dst = ml_send.at[:, pl.ds(base, size)], ml.at[y, :, pl.ds(base, size)]
            go(remote(src, dst, ml_ss.at[g, j], ml_rs.at[g, y], target))
        po[y, first:end] = po_send[first:end, y]
        ml[y, :, base : base + size] = ml_send[:, base : base + size]

    def pack_ml(packed_ml, h, peak, total, size):
        packed_ml = jnp.where(lane[0:size] == h, peak, packed_ml)
        return jnp.where(lane[0:size] == h + HPD, total, packed_ml)

    def attend_last(g):
        first, end = GROUPS[g]
        base, size = span_of(g)

        def head(h, packed_ml):
            peak, total, own = attend_keys(h, base, size, True)
            acc[h, pl.ds(base, size)] = own / total
            return pack_ml(packed_ml, h, peak, total, size)

        packed_ml = lax.fori_loop(0, HPD, head, jnp.zeros((size, 128), F32))
        for h in range(HPD):
            normal = acc[h, pl.ds(base, size)].astype(BF16)
            po_send[first:end, :, :, h * HD : (h + 1) * HD] = normal.reshape(end - first, NY, rows, HD)
        send_group(g, packed_ml)

    def finish_group(g):
        first, end = GROUPS[g]
        base, size = span_of(g)
        packed_ml = jnp.zeros((size, 128), F32)
        for h in range(HPD):
            s = dot_nt(queries[h, pl.ds(base, size)], fresh_k[h])
            old_peak = top[h, pl.ds(base, size)]
            peak = jnp.maximum(jnp.max(s, axis=1, keepdims=True), old_peak)
            w = jnp.exp2((s - jnp.concatenate([peak, peak], axis=1)) * SCALE)
            alpha = jnp.exp2((old_peak - peak) * SCALE)
            total = jnp.sum(w, axis=1, keepdims=True) + alpha * mass[h, pl.ds(base, size)]
            own = (dot(w.astype(BF16), fresh_v[h]) + alpha * acc[h, pl.ds(base, size)]) / total
            po_send[first:end, :, :, h * HD : (h + 1) * HD] = own.astype(BF16).reshape(end - first, NY, rows, HD)
            packed_ml = pack_ml(packed_ml, h, peak, total, size)
        send_group(g, packed_ml)

    def merge(g):
        first, end = GROUPS[g]
        base, size = span_of(g)
        mine = (end - first) * rows
        for j in range(1, NY):
            recv(ml.at[at_y(j), :, pl.ds(base, size)], ml_rs.at[g, at_y(j)])
            recv(po.at[at_y(j), pl.ds(first, end - first)], po_rs.at[g, at_y(j)])
        packed = jnp.concatenate([ml[yy, :, base : base + size] for yy in range(NY)] + [jnp.zeros((128 - NY * 8, size), F32)], axis=0)
        stats[first:end] = jnp.transpose(packed).reshape(end - first, NY, rows, 128)
        stat = stats[first:end, y].reshape(mine, 128)
        mixed = []
        for h in range(HPD):
            peaks = [stat[:, yy * 8 + h : yy * 8 + h + 1] for yy in range(NY)]
            totals = [stat[:, yy * 8 + HPD + h : yy * 8 + HPD + h + 1] for yy in range(NY)]
            peak = jnp.maximum(jnp.maximum(peaks[0], peaks[1]), jnp.maximum(peaks[2], peaks[3]))
            shares = [jnp.exp2((p - peak) * SCALE) * t for p, t in zip(peaks, totals)]
            whole = shares[0] + shares[1] + shares[2] + shares[3]
            own = sum(
                po[yy, first:end, :, h * HD : (h + 1) * HD].reshape(mine, HD).astype(F32) * (shares[yy] / whole)
                for yy in range(NY)
            )
            mixed.append((own + guest[h, first * rows : end * rows]).astype(BF16))
        ordered = dot(jnp.concatenate(mixed, axis=1), reorder[...]).astype(BF16)
        tile = 512

        def project_out(t, _):
            cols = pl.ds(pl.multiple_of(t * tile, tile), tile)
            w = woall[:, :, cols].reshape(NY * block, tile)
            part[first:end, :, cols] = dot(ordered, w).reshape(end - first, rows, tile)
            return 0

        lax.fori_loop(0, width // tile, project_out, 0)

    for yy, what, _, _ in streams[1:]:
        wait_hid(0, yy, what)
        send_hid(0, yy, what, up, -1)
        send_hid(0, yy, what, down, 1)
    for j, target in enumerate(peers):
        go(remote(gk.at[y], gk.at[y], gk_ss.at[j], gk_rs.at[y], target))
    send_wo(0)
    split_some(0, 6)
    for copy in w_copies:
        copy.wait()
    project(0)
    for k in range(1, 5):
        for yy, what, hops_up, hops_down in streams:
            for sign, hops, onward in ((-1, hops_up, up), (1, hops_down, down)):
                if k > hops:
                    continue
                d = sign * k
                wait_hid(d, yy, what)
                if k < hops:
                    send_hid(d, yy, what, onward, d + sign)
                if what == "r":
                    send_hid(d, yy, "c", right, d)
                    send_hid(d, yy, "d", left, d)
                if k == 4 and what == "r":
                    attend(3)
                    attend_guests(3)
        if k == 1:
            send_wo(1)
        if k == 2:
            pass_wo()
        if k == 1:
            split_some(6, 6, True)
            project(1)
            attend(0)
        if k == 2:
            project(2)
            attend(1)
            attend(2)
        if k == 3:
            project(3)
            for j in range(1, NY):
                recv(gk.at[at_y(j)], gk_rs.at[at_y(j)])
            for g in range(3):
                attend_guests(g)
    project(4)

    for g in range(5):
        first, end = GROUPS[g]
        for j in range(1, NY):
            recv(kvx.at[at_y(j), pl.ds(first, end - first)], kv_rs.at[g, at_y(j)])
    for s, fresh in enumerate((fresh_k, fresh_v)):
        both = sum(
            dot(kvx[yy, :, :, s * 128 : s * 128 + 128].reshape(line, 128), place[yy * 128 : yy * 128 + 128])
            for yy in range(NY)
        ).astype(BF16)
        for h in range(HPD):
            fresh[h] = both[:, h * HD : (h + 1) * HD]
    place_queries(4)
    attend_last(4)
    finish_group(3)
    attend_guests(4)
    own_wo.wait()
    for j, i in ((1, 0), (2, 0), (2, 1), (3, 1)):
        wait_wo(at_y(j), i)

    wide_tile = width // 4
    cols = [pl.ds(i * wide_tile, wide_tile) for i in range(4)]
    order = ((0, 0), (1, 1), (0, 2), (1, 3), (0, 1), (1, 0), (0, 3), (1, 2))
    for dist in (4, 3, 2, 1):
        merge(dist)
        for d, s in order:
            hops = 4 if d == s % 2 else 3
            if dist > hops:
                continue
            step = 1 if d == 0 else -1
            term = part[SLOT[step * dist], :, cols[s]]
            if dist < hops:
                recv(rs_recv.at[d, s, dist], rs_rs.at[d, s, dist])
                term = term + rs_recv[d, s, dist].astype(F32)
            rs_send[d, s, dist - 1] = term.astype(BF16)
            target = up if d == 0 else down
            n = dist - 1
            go(remote(rs_send.at[d, s, n], rs_recv.at[d, s, n], rs_ss.at[d, s, n], rs_rs.at[d, s, n], target))
        if dist > 1:
            finish_group(dist - 2)
    merge(0)
    for s in (0, 2, 1, 3):
        total = part[0, :, cols[s]]
        for d in range(2):
            recv(rs_recv.at[d, s, 0], rs_rs.at[d, s, 0])
            total = total + rs_recv[d, s, 0].astype(F32)
        gate = modul[2, :, cols[s]]
        res[s] = (act[:, cols[s]].astype(F32) + gate * total).astype(BF16)
        go(remote(res.at[s], out.at[:, cols[s]], res_ss.at[s], res_rs.at[s], (after, u)))
    for s in range(4):
        recv(out.at[:, cols[s]], res_rs.at[s])
    for copy in sends:
        copy.wait_send()


def shards(
    activations, patch_index, modulation, qkv_weight, out_weight, stale_cache, id_cache, region_ids, id_counts
):
    _, rows, width = activations.shape
    span = stale_cache.shape[2]
    slots = id_cache.shape[2] * id_cache.shape[3]
    line = NZ * rows
    tokens = NY * line
    block = qkv_weight.shape[2] // 3
    dma = pltpu.SemaphoreType.DMA
    vmem = pl.BlockSpec(memory_space=pltpu.VMEM)
    smem = pl.BlockSpec(memory_space=pltpu.SMEM)
    anywhere = pl.BlockSpec(memory_space=pl.ANY)
    result = pl.pallas_call(
        kernel,
        out_shape=jax.ShapeDtypeStruct((rows, width), BF16),
        in_specs=[vmem, vmem, smem, anywhere, anywhere, anywhere, vmem, vmem, smem],
        out_specs=vmem,
        scratch_shapes=[
            pltpu.VMEM((NZ, NY, rows, width + 128), BF16),
            pltpu.VMEM((3 * 128, width), BF16),
            pltpu.VMEM((2, 256, 2, HPD * HD), BF16),
            pltpu.VMEM((HPD, span, HD), BF16),
            pltpu.VMEM((HPD, span, HD), BF16),
            pltpu.VMEM((NZ, NY, rows, 3 * 128), BF16),
            pltpu.VMEM((NY, tokens, 128), BF16),
            pltpu.VMEM((NY, NZ, rows, 256), BF16),
            pltpu.VMEM((HPD, tokens, HD), BF16),
            pltpu.VMEM((HPD, line, HD), BF16),
            pltpu.VMEM((HPD, line, HD), BF16),
            pltpu.VMEM((HPD, tokens, HD), F32),
            pltpu.VMEM((HPD, tokens, 128), F32),
            pltpu.VMEM((HPD, tokens, 128), F32),
            pltpu.VMEM((NZ, NY, rows, HPD * HD), BF16),
            pltpu.VMEM((NY, NZ, rows, HPD * HD), BF16),
            pltpu.VMEM((8, tokens), F32),
            pltpu.VMEM((NY, 8, tokens), F32),
            pltpu.VMEM((NZ, NY, rows, 128), F32),
            pltpu.VMEM((HPD, line, HD), F32),
            pltpu.VMEM((NY, slots, 2 * HPD * HD), BF16),
            pltpu.VMEM((NY, block, width), BF16),
            pltpu.VMEM((NZ, rows, width), F32),
            pltpu.VMEM((2, 4, 4, rows, width // 4), BF16),
            pltpu.VMEM((2, 4, 4, rows, width // 4), BF16),
            pltpu.VMEM((4, rows, width // 4), BF16),
            pltpu.VMEM((NY * 128, HPD * HD), BF16),
            pltpu.VMEM((HPD * HD, NY * block), BF16),
            dma((64,)), dma((NZ, NY, 2)),
            dma((5, 3)), dma((5, NY)),
            dma((5, 3)), dma((5, NY)),
            dma((5, 3)), dma((5, NY)),
            dma((5, 3)), dma((5, NY)),
            dma((3,)), dma((NY,)),
            dma((3, 2)), dma((NY, 2)),
            dma,
            dma((2, 4, 4)), dma((2, 4, 4)),
            dma((4,)), dma((4,)),
            dma((2,)),
            dma((3,)),
        ],
        compiler_params=pltpu.CompilerParams(
            collective_id=0, has_side_effects=True, vmem_limit_bytes=56 * 2**20
        ),
        name="section",
    )(
        activations[0],
        jnp.transpose(modulation, (1, 0, 2)),
        patch_index,
        jnp.swapaxes(qkv_weight[0], 0, 1),
        out_weight[0],
        stale_cache[0, 0],
        id_cache[0, 0].reshape(slots, 2, HPD * HD),
        region_ids,
        id_counts,
    )
    return result[None]


def solution(mesh):
    placed = (
        P("pipe", "ulys", None),
        P("pipe"),
        P("pipe", None, None),
        P("pipe", None, "ulys"),
        P("pipe", "ulys", None),
        P("pipe", "ulys", None, None, None),
        P("pipe", "ulys", None, None, None, None),
        P("pipe", "ulys"),
        P("pipe", None),
    )
    return jax.shard_map(
        shards, mesh=mesh, in_specs=placed, out_specs=P("pipe", "ulys", None), check_vma=False
    )
```

time: 137 us -> 120 us (0.88)
  the two profiles are of different devices: /device:TPU:31 before, /device:TPU:1 now
where the time goes in v2:
time: 120 us
  Pallas kernels  118 us (98%)
  local copies, waits for them, and re-layouts  1.62 us (1%)
    pallas_call x1, Pallas kernels, shards(): pl.pallas_call(kernel, out_shape=jax.ShapeDtypeStruct((rows, width), BF16...  118 us

profile of v2, /device:TPU:1, one launch (start us, length us, event | category | flops | bytes accessed | tf_op | source)
XLA Modules:
  0.0 120.0 jit_solution(16742193195123294697)
XLA Ops:
  0.7 117.7 %section.1 = bf16[32,3072]{1,0:T(8,128)(2,1)} custom-call(bf16[32,3072]{1,0:T(8,128)(2,1)} %bitcast.13, f32[3,1,3072]{2,1,0:T(1,128)} %bitcast.15, s32[1]{0:T(128)S(6)} %copy.11.patch, bf16[288,3072]{1,0:T(8,128)(2,1)} %bitcast.10, bf16[96,3072]{1,0:T(8,128)(2,1)} %bitcast.12, bf16[3072,2,384]{2,1,0:T(2,128)(2,1)} %bitcast.9, bf16[48,2,384]{2,1,0:T(2,128)(2,1)} %bitcast.14, ...), custom_call_target="tpu_custom_call" | custom-call | tf_op jit(solution)/shard_map/section/pallas_call | solution.py:488
  118.3 1.6 %copy.12 = bf16[1,32,3072]{2,1,0:T(8,128)(2,1)} copy(bf16[1,32,3072]{2,1,0:T(8,128)(2,1)} %bitcast.11) | data formatting | bytes 393216

commit v3 on v2

--- a/solution.py
+++ b/solution.py
@@ -40,6 +40,7 @@
 ORDER = (0, -1, 1, -2, 2, -3, 3, 4)
 SLOT = {d: i for i, d in enumerate(ORDER)}
 SLOT[-4] = SLOT[4]
+NEAR = 2
 GROUPS = ((0, 1), (1, 3), (3, 5), (5, 7), (7, 8))
 
 
@@ -47,8 +48,8 @@
     act, modul, patch, wt, wo, cache, ids, region, counts,
     out,
     hid, wts, cbuf, keys, vals, pieces, qx, kvx, queries, fresh_k, fresh_v, acc, top, mass,
-    po_send, po, ml_send, ml, stats, guest, gk, woall, part, rs_send, rs_recv, res, place, reorder,
-    hid_ss, hid_rs, q_ss, q_rs, kv_ss, kv_rs, po_ss, po_rs, ml_ss, ml_rs,
+    po_send, po, guest, gk, woall, part, rs_send, rs_recv, res, place, reorder,
+    hid_ss, hid_rs, q_ss, q_rs, kv_ss, kv_rs, po_ss, po_rs,
     gk_ss, gk_rs, wo_ss, wo_rs, own_sem, rs_ss, rs_rs, res_ss, res_rs, c_sem, w_sem,
 ):
     pipe = lax.axis_index("pipe")
@@ -57,7 +58,7 @@
     rows, width = act.shape
     quad = NY * rows
     line = NZ * rows
-    split = (width * 3 // 4) // 128 * 128
+    split = width // 2
     span = cache.shape[0]
     chunk = span // 3
 
@@ -122,6 +123,12 @@
         copy.start()
         sends.append(copy)
 
+    def drain(keep=0):
+        done = sends[: len(sends) - keep]
+        del sends[: len(sends) - keep]
+        for copy in done:
+            copy.wait_send()
+
     def recv(ref, rs):
         remote(ref, ref, hid_ss.at[0], rs, dev(z, y)).wait_recv()
 
@@ -144,7 +151,11 @@
         cols, n = parts[what]
         recv(hid.at[SLOT[d], yy, :, cols], hid_rs.at[SLOT[d], yy, n])
 
-    streams = ((y, "r", 4, 3), (at_y(1), "a", 4, 3), (at_y(3), "b", 3, 4), (at_y(2), "w", 3, 4))
+    streams = ((y, "r", 4, 3), (at_y(2), "w", 3, 4), (at_y(1), "a", 4, 3), (at_y(3), "b", 3, 4))
+    lateral = {"a": "d", "b": "c"}
+
+    def part_at(what, k):
+        return "w" if what in lateral and k > NEAR else what
 
     wo_half = [pl.ds(i * (block // 2), block // 2) for i in range(2)]
 
@@ -206,8 +217,9 @@
     def project(g):
         first, end = GROUPS[g]
         for d in ORDER[first:end]:
-            wait_hid(d, at_y(3), "c")
-            wait_hid(d, at_y(1), "d")
+            if abs(d) < NEAR:
+                wait_hid(d, at_y(3), "c")
+                wait_hid(d, at_y(1), "d")
         base, size = span_of(g)
         x = hid[first:end, :, :, 0:width].reshape(size, width)
         p = dot_nt(x, wts[...]).astype(BF16)
@@ -230,6 +242,21 @@
         full = sum(dot(qx[yy, pl.ds(base, size)], place[yy * 128 : yy * 128 + 128]) for yy in range(NY)).astype(BF16)
         for h in range(HPD):
             queries[h, pl.ds(base, size)] = full[:, h * HD : (h + 1) * HD]
+
+    def place_fresh(g_first, g_end):
+        for g in range(g_first, g_end):
+            first, end = GROUPS[g]
+            for j in range(1, NY):
+                recv(kvx.at[at_y(j), pl.ds(first, end - first)], kv_rs.at[g, at_y(j)])
+        first, end = GROUPS[g_first][0], GROUPS[g_end - 1][1]
+        size = (end - first) * rows
+        for s, fresh in enumerate((fresh_k, fresh_v)):
+            both = sum(
+                dot(kvx[yy, first:end, :, s * 128 : s * 128 + 128].reshape(size, 128), place[yy * 128 : yy * 128 + 128])
+                for yy in range(NY)
+            ).astype(BF16)
+            for h in range(HPD):
+                fresh[h, first * rows : end * rows] = both[:, h * HD : (h + 1) * HD]
 
     def attend_keys(h, base, size, with_fresh):
         q = queries[h, pl.ds(base, size)]
@@ -252,9 +279,10 @@
             own = own + dot(w.astype(BF16), fresh_v[h])
         return peak, total, own
 
-    def attend(g):
+    def attend(g, h_first=0, h_end=HPD):
         base, size = span_of(g)
-        place_queries(g)
+        if h_first == 0:
+            place_queries(g)
 
         def head(h, _):
             peak, total, own = attend_keys(h, base, size, False)
@@ -263,7 +291,7 @@
             mass[h, pl.ds(base, size)] = jnp.broadcast_to(total, (size, 128))
             return 0
 
-        lax.fori_loop(0, HPD, head, 0)
+        lax.fori_loop(h_first, h_end, head, 0)
 
     total_slots = NY * slots
     per_subject = slots // SUBJ
@@ -293,16 +321,15 @@
 
     def send_group(g, packed_ml):
         first, end = GROUPS[g]
-        base, size = span_of(g)
+        high = packed_ml.astype(BF16).astype(F32)
+        middle = (packed_ml - high).astype(BF16).astype(F32)
+        low = packed_ml - high - middle
+        spread = high + pltpu.roll(middle, 2 * HPD, 1) + pltpu.roll(low, 4 * HPD, 1)
+        po_send[first:end, :, :, HPD * HD :] = spread.astype(BF16).reshape(end - first, NY, rows, 128)
         for j, target in enumerate(peers):
             src = po_send.at[pl.ds(first, end - first), at_y(j + 1)]
             go(remote(src, po.at[y, pl.ds(first, end - first)], po_ss.at[g, j], po_rs.at[g, y], target))
-        ml_send[:, base : base + size] = jnp.transpose(packed_ml)[0:8]
-        for j, target in enumerate(peers):
-            src, dst = ml_send.at[:, pl.ds(base, size)], ml.at[y, :, pl.ds(base, size)]
-            go(remote(src, dst, ml_ss.at[g, j], ml_rs.at[g, y], target))
         po[y, first:end] = po_send[first:end, y]
-        ml[y, :, base : base + size] = ml_send[:, base : base + size]
 
     def pack_ml(packed_ml, h, peak, total, size):
         packed_ml = jnp.where(lane[0:size] == h, peak, packed_ml)
@@ -312,15 +339,12 @@
         first, end = GROUPS[g]
         base, size = span_of(g)
 
-        def head(h, packed_ml):
+        packed_ml = jnp.zeros((size, 128), F32)
+        for h in range(HPD):
             peak, total, own = attend_keys(h, base, size, True)
-            acc[h, pl.ds(base, size)] = own / total
-            return pack_ml(packed_ml, h, peak, total, size)
-
-        packed_ml = lax.fori_loop(0, HPD, head, jnp.zeros((size, 128), F32))
-        for h in range(HPD):
-            normal = acc[h, pl.ds(base, size)].astype(BF16)
+            normal = (own / total).astype(BF16)
             po_send[first:end, :, :, h * HD : (h + 1) * HD] = normal.reshape(end - first, NY, rows, HD)
+            packed_ml = pack_ml(packed_ml, h, peak, total, size)
         send_group(g, packed_ml)
 
     def finish_group(g):
@@ -344,95 +368,89 @@
         base, size = span_of(g)
         mine = (end - first) * rows
         for j in range(1, NY):
-            recv(ml.at[at_y(j), :, pl.ds(base, size)], ml_rs.at[g, at_y(j)])
             recv(po.at[at_y(j), pl.ds(first, end - first)], po_rs.at[g, at_y(j)])
-        packed = jnp.concatenate([ml[yy, :, base : base + size] for yy in range(NY)] + [jnp.zeros((128 - NY * 8, size), F32)], axis=0)
-        stats[first:end] = jnp.transpose(packed).reshape(end - first, NY, rows, 128)
-        stat = stats[first:end, y].reshape(mine, 128)
+        peaks, totals = [], []
+        for yy in range(NY):
+            spread = po[yy, first:end, :, HPD * HD :].reshape(mine, 128).astype(F32)
+            stat = spread + pltpu.roll(spread, 128 - 2 * HPD, 1) + pltpu.roll(spread, 128 - 4 * HPD, 1)
+            used = lane[0:mine] < HPD
+            peaks.append(jnp.where(used, stat, 0.0))
+            totals.append(jnp.where(used, pltpu.roll(stat, 128 - HPD, 1), 1.0))
+        peak = jnp.maximum(jnp.maximum(peaks[0], peaks[1]), jnp.maximum(peaks[2], peaks[3]))
+        shares = [jnp.exp2((p - peak) * SCALE) * t for p, t in zip(peaks, totals)]
+        inverse = 1.0 / (shares[0] + shares[1] + shares[2] + shares[3])
+        shares = [share * inverse for share in shares]
         mixed = []
         for h in range(HPD):
-            peaks = [stat[:, yy * 8 + h : yy * 8 + h + 1] for yy in range(NY)]
-            totals = [stat[:, yy * 8 + HPD + h : yy * 8 + HPD + h + 1] for yy in range(NY)]
-            peak = jnp.maximum(jnp.maximum(peaks[0], peaks[1]), jnp.maximum(peaks[2], peaks[3]))
-            shares = [jnp.exp2((p - peak) * SCALE) * t for p, t in zip(peaks, totals)]
-            whole = shares[0] + shares[1] + shares[2] + shares[3]
             own = sum(
-                po[yy, first:end, :, h * HD : (h + 1) * HD].reshape(mine, HD).astype(F32) * (shares[yy] / whole)
+                po[yy, first:end, :, h * HD : (h + 1) * HD].reshape(mine, HD).astype(F32) * shares[yy][:, h : h + 1]
                 for yy in range(NY)
             )
             mixed.append((own + guest[h, first * rows : end * rows]).astype(BF16))
         ordered = dot(jnp.concatenate(mixed, axis=1), reorder[...]).astype(BF16)
         tile = 512
 
-        def project_out(t, _):
-            cols = pl.ds(pl.multiple_of(t * tile, tile), tile)
+        for t in range(width // tile):
+            cols = pl.ds(t * tile, tile)
             w = woall[:, :, cols].reshape(NY * block, tile)
             part[first:end, :, cols] = dot(ordered, w).reshape(end - first, rows, tile)
-            return 0
-
-        lax.fori_loop(0, width // tile, project_out, 0)
-
-    for yy, what, _, _ in streams[1:]:
+
+    for yy, what, _, _ in (streams[2], streams[3], streams[1]):
         wait_hid(0, yy, what)
         send_hid(0, yy, what, up, -1)
         send_hid(0, yy, what, down, 1)
     for j, target in enumerate(peers):
         go(remote(gk.at[y], gk.at[y], gk_ss.at[j], gk_rs.at[y], target))
     send_wo(0)
-    split_some(0, 6)
+    split_some(0, 4)
     for copy in w_copies:
         copy.wait()
     project(0)
+
+    def late_guests():
+        for j in range(1, NY):
+            recv(gk.at[at_y(j)], gk_rs.at[at_y(j)])
+        attend_guests(0)
+
+    work = {
+        (1, 0): [ lambda: split_some(4, 4)],
+        (1, 1): [lambda: split_some(8, 4, True)],
+        (2, 0): [lambda: project(1)],
+        (2, 1): [lambda: attend(0)],
+        (2, 3): [lambda: send_wo(1), lambda: attend(1, 0, 2)],
+        (3, 0): [lambda: project(2), lambda: attend(1, 2, 3)],
+        (3, 1): [late_guests, lambda: attend_guests(1)],
+        (3, 2): [lambda: attend(2, 0, 2)],
+        (3, 3): [lambda: project(3), pass_wo, lambda: attend(2, 2, 3), lambda: attend_guests(2), lambda: attend(3, 0, 2)],
+    }
     for k in range(1, 5):
-        for yy, what, hops_up, hops_down in streams:
+        before_step = len(sends)
+        for i, (yy, what, hops_up, hops_down) in enumerate(streams):
             for sign, hops, onward in ((-1, hops_up, up), (1, hops_down, down)):
                 if k > hops:
                     continue
                 d = sign * k
-                wait_hid(d, yy, what)
+                wait_hid(d, yy, part_at(what, k))
+                if k == NEAR and what in lateral:
+                    wait_hid(d, yy, lateral[what])
                 if k < hops:
-                    send_hid(d, yy, what, onward, d + sign)
-                if what == "r":
+                    send_hid(d, yy, part_at(what, k + 1), onward, d + sign)
+                if k <= NEAR and what == "r":
                     send_hid(d, yy, "c", right, d)
                     send_hid(d, yy, "d", left, d)
-                if k == 4 and what == "r":
-                    attend(3)
-                    attend_guests(3)
-        if k == 1:
-            send_wo(1)
-        if k == 2:
-            pass_wo()
-        if k == 1:
-            split_some(6, 6, True)
-            project(1)
-            attend(0)
-        if k == 2:
-            project(2)
-            attend(1)
-            attend(2)
-        if k == 3:
-            project(3)
-            for j in range(1, NY):
-                recv(gk.at[at_y(j)], gk_rs.at[at_y(j)])
-            for g in range(3):
-                attend_guests(g)
+            for task in work.get((k, i), ()):
+                task()
     project(4)
-
-    for g in range(5):
-        first, end = GROUPS[g]
-        for j in range(1, NY):
-            recv(kvx.at[at_y(j), pl.ds(first, end - first)], kv_rs.at[g, at_y(j)])
-    for s, fresh in enumerate((fresh_k, fresh_v)):
-        both = sum(
-            dot(kvx[yy, :, :, s * 128 : s * 128 + 128].reshape(line, 128), place[yy * 128 : yy * 128 + 128])
-            for yy in range(NY)
-        ).astype(BF16)
-        for h in range(HPD):
-            fresh[h] = both[:, h * HD : (h + 1) * HD]
+    drain(20)
+    attend(3, 2, 3)
+    attend_guests(3)
+    place_fresh(0, 4)
+    place_fresh(4, 5)
     place_queries(4)
     attend_last(4)
     finish_group(3)
     attend_guests(4)
+    drain(6)
     own_wo.wait()
     for j, i in ((1, 0), (2, 0), (2, 1), (3, 1)):
         wait_wo(at_y(j), i)
@@ -466,10 +484,9 @@
         gate = modul[2, :, cols[s]]
         res[s] = (act[:, cols[s]].astype(F32) + gate * total).astype(BF16)
         go(remote(res.at[s], out.at[:, cols[s]], res_ss.at[s], res_rs.at[s], (after, u)))
+    drain()
     for s in range(4):
         recv(out.at[:, cols[s]], res_rs.at[s])
-    for copy in sends:
-        copy.wait_send()
 
 
 def shards(
@@ -505,11 +522,8 @@
             pltpu.VMEM((HPD, tokens, HD), F32),
             pltpu.VMEM((HPD, tokens, 128), F32),
             pltpu.VMEM((HPD, tokens, 128), F32),
-            pltpu.VMEM((NZ, NY, rows, HPD * HD), BF16),
-            pltpu.VMEM((NY, NZ, rows, HPD * HD), BF16),
-            pltpu.VMEM((8, tokens), F32),
-            pltpu.VMEM((NY, 8, tokens), F32),
-            pltpu.VMEM((NZ, NY, rows, 128), F32),
+            pltpu.VMEM((NZ, NY, rows, (HPD + 1) * HD), BF16),
+            pltpu.VMEM((NY, NZ, rows, (HPD + 1) * HD), BF16),
             pltpu.VMEM((HPD, line, HD), F32),
             pltpu.VMEM((NY, slots, 2 * HPD * HD), BF16),
             pltpu.VMEM((NY, block, width), BF16),
@@ -520,7 +534,6 @@
             pltpu.VMEM((NY * 128, HPD * HD), BF16),
             pltpu.VMEM((HPD * HD, NY * block), BF16),
             dma((64,)), dma((NZ, NY, 2)),
-            dma((5, 3)), dma((5, NY)),
             dma((5, 3)), dma((5, NY)),
             dma((5, 3)), dma((5, NY)),
             dma((5, 3)), dma((5, NY)),

time: 120 us -> 108 us (0.900)
  Pallas kernels: 118 us -> 105 us
    pallas_call x1, Pallas kernels: 118 us -> 105 us  [shards(): pl.pallas_call(kernel, out_shape=jax.ShapeDtypeStruct((rows, width), BF16...]
where the time goes in v3:
time: 108 us
  Pallas kernels  105 us (97%)
  local copies, waits for them, and re-layouts  1.62 us (2%)
    pallas_call x1, Pallas kernels, shards(): pl.pallas_call(kernel, out_shape=jax.ShapeDtypeStruct((rows, width), BF16...  105 us

profile of v3, /device:TPU:1, one launch (start us, length us, event | category | flops | bytes accessed | tf_op | source)
XLA Modules:
  0.0 107.5 jit_solution(10220822013932107140)
XLA Ops:
  0.7 105.3 %section.1 = bf16[32,3072]{1,0:T(8,128)(2,1)} custom-call(bf16[32,3072]{1,0:T(8,128)(2,1)} %bitcast.13, f32[3,1,3072]{2,1,0:T(1,128)} %bitcast.15, s32[1]{0:T(128)S(6)} %copy.11.patch, bf16[288,3072]{1,0:T(8,128)(2,1)} %bitcast.10, bf16[96,3072]{1,0:T(8,128)(2,1)} %bitcast.12, bf16[3072,2,384]{2,1,0:T(2,128)(2,1)} %bitcast.9, bf16[48,2,384]{2,1,0:T(2,128)(2,1)} %bitcast.14, ...), custom_call_target="tpu_custom_call" | custom-call | tf_op jit(solution)/shard_map/section/pallas_call | solution.py:505
  105.9 1.6 %copy.12 = bf16[1,32,3072]{2,1,0:T(8,128)(2,1)} copy(bf16[1,32,3072]{2,1,0:T(8,128)(2,1)} %bitcast.11) | data formatting | bytes 393216

commit v4 on v3

--- a/solution.py
+++ b/solution.py
@@ -417,11 +417,11 @@
         (1, 1): [lambda: split_some(8, 4, True)],
         (2, 0): [lambda: project(1)],
         (2, 1): [lambda: attend(0)],
-        (2, 3): [lambda: send_wo(1), lambda: attend(1, 0, 2)],
-        (3, 0): [lambda: project(2), lambda: attend(1, 2, 3)],
+        (2, 3): [lambda: attend(1, 0, 2)],
+        (3, 0): [lambda: project(2), lambda: send_wo(1), lambda: attend(1, 2, 3)],
         (3, 1): [late_guests, lambda: attend_guests(1)],
         (3, 2): [lambda: attend(2, 0, 2)],
-        (3, 3): [lambda: project(3), pass_wo, lambda: attend(2, 2, 3), lambda: attend_guests(2), lambda: attend(3, 0, 2)],
+        (3, 3): [lambda: project(3), lambda: attend(2, 2, 3), lambda: attend_guests(2), lambda: attend(3, 0, 2)],
     }
     for k in range(1, 5):
         before_step = len(sends)
@@ -441,6 +441,7 @@
             for task in work.get((k, i), ()):
                 task()
     project(4)
+    pass_wo()
     drain(20)
     attend(3, 2, 3)
     attend_guests(3)

time: 108 us -> 106 us (0.981)
    pallas_call x1, Pallas kernels: 105 us -> 104 us  [shards(): pl.pallas_call(kernel, out_shape=jax.ShapeDtypeStruct((rows, width), BF16...]
where the time goes in v4:
time: 106 us
  Pallas kernels  104 us (98%)
  local copies, waits for them, and re-layouts  1.62 us (2%)
    pallas_call x1, Pallas kernels, shards(): pl.pallas_call(kernel, out_shape=jax.ShapeDtypeStruct((rows, width), BF16...  104 us

profile of v4, /device:TPU:1, one launch (start us, length us, event | category | flops | bytes accessed | tf_op | source)
XLA Modules:
  0.0 106.1 jit_solution(13522879317445400552)
XLA Ops:
  0.7 103.8 %section.1 = bf16[32,3072]{1,0:T(8,128)(2,1)} custom-call(bf16[32,3072]{1,0:T(8,128)(2,1)} %bitcast.13, f32[3,1,3072]{2,1,0:T(1,128)} %bitcast.15, s32[1]{0:T(128)S(6)} %copy.11.patch, bf16[288,3072]{1,0:T(8,128)(2,1)} %bitcast.10, bf16[96,3072]{1,0:T(8,128)(2,1)} %bitcast.12, bf16[3072,2,384]{2,1,0:T(2,128)(2,1)} %bitcast.9, bf16[48,2,384]{2,1,0:T(2,128)(2,1)} %bitcast.14, ...), custom_call_target="tpu_custom_call" | custom-call | tf_op jit(solution)/shard_map/section/pallas_call | solution.py:506
  104.5 1.6 %copy.12 = bf16[1,32,3072]{2,1,0:T(8,128)(2,1)} copy(bf16[1,32,3072]{2,1,0:T(8,128)(2,1)} %bitcast.11) | data formatting | bytes 393216
